TPU v7x, 32 devices: a whole 2x2x4 slice. The times are simulated.
32 devices in a mesh: dp: 4 (over z), row: 4 (over y, x), col: 2 (over core).
Axes of the slice: x: 2, y: 2, z: 4, core: 2. Of those that a mesh axis runs over, the one named last changes fastest.
Arguments:
- inputs: bfloat16 [4096, 2048], P('dp'), may hold values from -6 to 6
- segments: int32 [4, 1024], P('dp'), may hold values from 0 to 5, never falling along the last dimension, each value on 1 to 768 neighbouring positions
- mixer_gain: float32 [2048], replicated, may hold values from 0.5 to 1.5
- w_query: bfloat16 [2048, 2048], P('col', 'row'), may hold values from -0.125 to 0.125
- w_key: bfloat16 [2048, 2048], P('col', 'row'), may hold values from -0.125 to 0.125
- w_value: bfloat16 [2048, 2048], P('col', 'row'), may hold values from -0.125 to 0.125
- w_beta: bfloat16 [2048, 16], P('col', 'row'), may hold values from -0.125 to 0.125
- conv_query: float32 [2048, 4], P(('row', 'col')), may hold values from -3 to 3
- conv_key: float32 [2048, 4], P(('row', 'col')), may hold values from -3 to 3
- conv_value: float32 [2048, 4], P(('row', 'col')), may hold values from -3 to 3
- head_gain: float32 [128], replicated, may hold values from 0.5 to 1.5
- w_out: bfloat16 [2048, 2048], P('row', 'col'), may hold values from -0.125 to 0.125
- feed_gain: float32 [2048], replicated, may hold values from 0.5 to 1.5
- w_gate: bfloat16 [2048, 5632], P('col', 'row'), may hold values from -0.125 to 0.125
- w_up: bfloat16 [2048, 5632], P('col', 'row'), may hold values from -0.125 to 0.125
- w_down: bfloat16 [5632, 2048], P('row', 'col'), may hold values from -0.078125 to 0.078125
- cotangent: bfloat16 [4096, 2048], P('dp'), may hold values from -6 to 6
Outputs:
- output: bfloat16 [4096, 2048], P('dp')
- input_grad: bfloat16 [4096, 2048], P('dp')
- mixer_gain_grad: float32 [2048], P('dp')
- query_grad: float32 [2048, 2048], P(('col', 'dp'), 'row')
- key_grad: float32 [2048, 2048], P(('col', 'dp'), 'row')
- value_grad: float32 [2048, 2048], P(('col', 'dp'), 'row')
- beta_grad: float32 [2048, 16], P(('col', 'dp'), 'row')
- conv_query_grad: float32 [2048, 4], P(('row', 'col', 'dp'))
- conv_key_grad: float32 [2048, 4], P(('row', 'col', 'dp'))
- conv_value_grad: float32 [2048, 4], P(('row', 'col', 'dp'))
- head_gain_grad: float32 [128], replicated
- out_grad: float32 [2048, 2048], P(('row', 'dp'), 'col')
- feed_gain_grad: float32 [2048], P('dp')
- gate_grad: float32 [2048, 5632], P(('col', 'dp'), 'row')
- up_grad: float32 [2048, 5632], P(('col', 'dp'), 'row')
- down_grad: float32 [5632, 2048], P(('row', 'dp'), 'col')
Inputs may be any that keep to these rules, and one draw needn't show every extreme that they name: `segments`: along each sequence the numbers never fall and begin at 0; a document has at most 768 tokens, and one of each sequence has exactly that many.
All inputs are finite; a program needn't handle non-finite values.
Results may differ from a plain program's by a relative error of at most 0.017.
Values may be sent and summed in bfloat16 or wider, within the bound.
No kernel may reach another device: no remote copies, remote signals or barrier semaphores. Data moves between devices by JAX's collectives and lax.ppermute only.
A program may use at most 192 MiB of HBM per device.

v0:
```python
import jax
import jax.numpy as jnp
from jax import lax
from jax.sharding import PartitionSpec as P

SPAN = 64
LEN = 1024


EPSILON = 1e-06
HEAD_FLOOR = 0.02
PRECISE = lax.Precision.HIGHEST


def rms_rows(values, scales):
    mean_square = jnp.mean(values * values, axis=-1, keepdims=True)
    return values * lax.rsqrt(mean_square + EPSILON) * scales


def head_rms(values, scales):
    mean_square = jnp.mean(values * values, axis=-1, keepdims=True)
    return values * lax.rsqrt(mean_square + HEAD_FLOOR) * scales


def causal_conv(values, kernel, documents):
    taps_count = kernel.shape[1]
    result = values * kernel[:, taps_count - 1]
    for offset in range(1, taps_count):
        shifted = jnp.concatenate(
            [jnp.zeros((offset, values.shape[1]), jnp.float32), values[:-offset]], 0
        )
        earlier = jnp.concatenate([jnp.full((offset,), -1, jnp.int32), documents[:-offset]], 0)
        result = (
            result
            + jnp.where((earlier == documents)[:, None], shifted, 0.0)
            * kernel[:, taps_count - 1 - offset]
        )
    return result


def span_step(memory, block_item):
    queries, key_vecs, values, strengths, documents, previous = block_item
    query_heads = jnp.transpose(queries, (1, 0, 2))
    key_heads = jnp.transpose(key_vecs, (1, 0, 2))
    value_heads = jnp.transpose(values, (1, 0, 2))
    beta_heads = jnp.transpose(strengths, (1, 0))
    length = documents.shape[0]
    places = jnp.arange(length, dtype=jnp.int32)
    same_doc = (documents[:, None] == documents[None, :]).astype(jnp.float32)
    earlier = (places[:, None] > places[None, :]).astype(jnp.float32)
    inclusive = (places[:, None] >= places[None, :]).astype(jnp.float32)
    carried = (documents == previous).astype(jnp.float32)
    key_gram = jnp.einsum("hik,hjk->hij", key_heads, key_heads, precision=PRECISE)
    system = (
        jnp.eye(length, dtype=jnp.float32)[None]
        + beta_heads[:, :, None] * key_gram * (same_doc * earlier)[None]
    )
    recalled = jnp.einsum("hck,hvk->hcv", key_heads, memory, precision=PRECISE)
    target = beta_heads[:, :, None] * (value_heads - carried[None, :, None] * recalled)
    writes = lax.linalg.triangular_solve(system, target, left_side=True, lower=True)
    scores = (
        jnp.einsum("hik,hjk->hij", query_heads, key_heads, precision=PRECISE)
        * (same_doc * inclusive)[None]
    )
    read_old = jnp.einsum("hck,hvk->hcv", query_heads, memory, precision=PRECISE)
    outputs = carried[None, :, None] * read_old + jnp.einsum(
        "hij,hjv->hiv", scores, writes, precision=PRECISE
    )
    closing = (documents == documents[length - 1]).astype(jnp.float32)
    new_memory = carried[length - 1] * memory + jnp.einsum(
        "hcv,hck->hvk", writes * closing[None, :, None], key_heads, precision=PRECISE
    )
    return (new_memory, jnp.transpose(outputs, (1, 0, 2)))


def delta_rule(queries, key_vecs, values, strengths, documents):
    tokens, head_count, head_size = queries.shape
    blocks = tokens // SPAN
    preceding = jnp.concatenate([jnp.full((1,), -1, jnp.int32), documents[:-1]], 0)
    start_memory = jnp.zeros((head_count, values.shape[2], head_size), jnp.float32)
    final_memory, outputs = lax.scan(
        jax.checkpoint(span_step),
        start_memory,
        (
            queries.reshape(blocks, SPAN, head_count, head_size),
            key_vecs.reshape(blocks, SPAN, head_count, head_size),
            values.reshape(blocks, SPAN, head_count, -1),
            strengths.reshape(blocks, SPAN, head_count),
            documents.reshape(blocks, SPAN),
            preceding.reshape(blocks, SPAN)[:, 0],
        ),
    )
    return outputs.reshape(tokens, head_count, -1)


def mixer_heads(
    query_in, key_in, value_in, beta_in, query_kernel, key_kernel, value_kernel, scales, documents
):
    tokens = query_in.shape[0]
    head_count = beta_in.shape[1]
    head_size = scales.shape[0]
    queries = jax.nn.silu(causal_conv(query_in, query_kernel, documents)).reshape(
        tokens, head_count, head_size
    )
    key_vecs = jax.nn.silu(causal_conv(key_in, key_kernel, documents)).reshape(
        tokens, head_count, head_size
    )
    key_vecs = key_vecs * lax.rsqrt(jnp.sum(key_vecs * key_vecs, axis=-1, keepdims=True) + EPSILON)
    values = jax.nn.silu(causal_conv(value_in, value_kernel, documents)).reshape(
        tokens, head_count, head_size
    )
    strengths = jax.nn.sigmoid(beta_in)
    mixed = delta_rule(queries, key_vecs, values, strengths, documents)
    return head_rms(mixed, scales).reshape(tokens, head_count * head_size)


def silu_product(gate_value, up_value):
    return jax.nn.silu(gate_value) * up_value


def matmul(left, right):
    return jnp.dot(left, right, preferred_element_type=jnp.float32)


def left_contract(left, right):
    return lax.dot_general(
        left, right, (((0,), (0,)), ((), ())), preferred_element_type=jnp.float32
    )


def right_contract(left, right):
    return lax.dot_general(
        left, right, (((1,), (1,)), ((), ())), preferred_element_type=jnp.float32
    )


def grid_total(partial_value):
    summed = lax.psum(partial_value, "row")
    return lax.all_gather(summed, "col", axis=1, tiled=True)


def token_sum(term_maker, row_total):
    return lax.psum_scatter(
        term_maker(jnp.int32(0), row_total * lax.axis_size("col")),
        "col",
        scatter_dimension=0,
        tiled=True,
    )


def token_gather(values):
    return lax.all_gather(values, "col", axis=0, tiled=True)


def body(
    inputs,
    segments,
    mixer_gain,
    w_query,
    w_key,
    w_value,
    w_beta,
    conv_query,
    conv_key,
    conv_value,
    head_gain,
    w_out,
    feed_gain,
    w_gate,
    w_up,
    w_down,
    cotangent,
):
    col_devices = lax.axis_size("col")
    residual = inputs.astype(jnp.float32)
    token_count, full_width = residual.shape
    half_width = full_width // col_devices
    col_start = lax.axis_index("col") * half_width
    row_half = token_count // col_devices
    documents = (
        segments + (jnp.arange(segments.shape[0], dtype=jnp.int32) * LEN)[:, None]
    ).reshape(-1)
    normed, norm_one_back = jax.vjp(rms_rows, residual, mixer_gain)
    action = normed.astype(jnp.bfloat16)
    action_mine = lax.dynamic_slice_in_dim(action, col_start, half_width, 1)
    query_in, key_in, value_in, beta_in = (
        lax.psum_scatter(matmul(action_mine, w_query), "col", scatter_dimension=1, tiled=True),
        lax.psum_scatter(matmul(action_mine, w_key), "col", scatter_dimension=1, tiled=True),
        lax.psum_scatter(matmul(action_mine, w_value), "col", scatter_dimension=1, tiled=True),
        lax.psum_scatter(matmul(action_mine, w_beta), "col", scatter_dimension=1, tiled=True),
    )

    def head_block(
        query_part, key_part, value_part, beta_part, query_kernel, key_kernel, value_kernel, scales
    ):
        return mixer_heads(
            query_part,
            key_part,
            value_part,
            beta_part,
            query_kernel,
            key_kernel,
            value_kernel,
            scales,
            documents,
        )

    head_values, heads_back = jax.vjp(
        head_block, query_in, key_in, value_in, beta_in, conv_query, conv_key, conv_value, head_gain
    )
    head_rows = lax.all_gather(head_values.astype(jnp.bfloat16), "col", axis=1, tiled=True)
    attended = grid_total(matmul(head_rows, w_out))
    middle = residual + attended
    normed_two, norm_two_back = jax.vjp(rms_rows, middle, feed_gain)
    action_two = normed_two.astype(jnp.bfloat16)
    action_two_mine = lax.dynamic_slice_in_dim(action_two, col_start, half_width, 1)
    feed_local = w_gate.shape[1]

    def gate_term(offset, amount):
        return jnp.concatenate([matmul(action_two_mine, w_gate), matmul(action_two_mine, w_up)], 1)

    gate_up = token_sum(gate_term, row_half)
    swiglu, swiglu_back = jax.vjp(silu_product, gate_up[:, :feed_local], gate_up[:, feed_local:])
    hidden_rows = token_gather(swiglu.astype(jnp.bfloat16))
    feed_out = grid_total(matmul(hidden_rows, w_down))
    output = (middle + feed_out).astype(jnp.bfloat16)
    upstream = cotangent.astype(jnp.float32)
    upstream_mine = lax.dynamic_slice_in_dim(cotangent, col_start, half_width, 1)

    def down_term(offset, amount):
        return right_contract(upstream_mine, w_down)

    hidden_grad = token_sum(down_term, row_half)
    down_grad = left_contract(hidden_rows, upstream_mine)
    gate_part, up_part = swiglu_back(hidden_grad)
    gate_up_rows = token_gather(jnp.concatenate([gate_part, up_part], 1).astype(jnp.bfloat16))
    gate_rows = gate_up_rows[:, :feed_local]
    up_rows = gate_up_rows[:, feed_local:]
    gate_grad = left_contract(action_two_mine, gate_rows)
    up_grad = left_contract(action_two_mine, up_rows)
    action_two_grad = grid_total(right_contract(gate_rows, w_gate) + right_contract(up_rows, w_up))
    middle_part, feed_part = norm_two_back(action_two_grad)
    middle_grad = middle_part + upstream
    attended_mine = lax.dynamic_slice_in_dim(
        middle_grad.astype(jnp.bfloat16), col_start, half_width, 1
    )
    out_grad = left_contract(head_rows, attended_mine)
    head_grad = lax.psum_scatter(
        right_contract(attended_mine, w_out).astype(jnp.bfloat16),
        "col",
        scatter_dimension=1,
        tiled=True,
    ).astype(jnp.float32)
    (
        query_part,
        key_part,
        value_part,
        beta_part,
        query_kernel_grad,
        key_kernel_grad,
        value_kernel_grad,
        scale_grad,
    ) = heads_back(head_grad)
    query_rows, key_rows, value_rows, beta_rows = (
        lax.all_gather(query_part.astype(jnp.bfloat16), "col", axis=1, tiled=True),
        lax.all_gather(key_part.astype(jnp.bfloat16), "col", axis=1, tiled=True),
        lax.all_gather(value_part.astype(jnp.bfloat16), "col", axis=1, tiled=True),
        lax.all_gather(beta_part.astype(jnp.bfloat16), "col", axis=1, tiled=True),
    )
    query_grad = left_contract(action_mine, query_rows)
    key_grad = left_contract(action_mine, key_rows)
    value_grad = left_contract(action_mine, value_rows)
    beta_grad = left_contract(action_mine, beta_rows)
    action_grad = grid_total(
        right_contract(query_rows, w_query)
        + right_contract(key_rows, w_key)
        + right_contract(value_rows, w_value)
        + right_contract(beta_rows, w_beta)
    )
    input_part, mixer_part = norm_one_back(action_grad)
    input_grad = (input_part + middle_grad).astype(jnp.bfloat16)
    head_gain_grad = lax.psum(scale_grad, ("dp", "row", "col"))
    every_grad = (
        lax.psum_scatter(
            mixer_part.astype(jnp.bfloat16), "dp", scatter_dimension=0, tiled=True
        ).astype(jnp.float32),
        lax.psum_scatter(
            query_grad.astype(jnp.bfloat16), "dp", scatter_dimension=0, tiled=True
        ).astype(jnp.float32),
        lax.psum_scatter(
            key_grad.astype(jnp.bfloat16), "dp", scatter_dimension=0, tiled=True
        ).astype(jnp.float32),
        lax.psum_scatter(
            value_grad.astype(jnp.bfloat16), "dp", scatter_dimension=0, tiled=True
        ).astype(jnp.float32),
        lax.psum_scatter(
            beta_grad.astype(jnp.bfloat16), "dp", scatter_dimension=0, tiled=True
        ).astype(jnp.float32),
        lax.psum_scatter(
            query_kernel_grad.astype(jnp.bfloat16), "dp", scatter_dimension=0, tiled=True
        ).astype(jnp.float32),
        lax.psum_scatter(
            key_kernel_grad.astype(jnp.bfloat16), "dp", scatter_dimension=0, tiled=True
        ).astype(jnp.float32),
        lax.psum_scatter(
            value_kernel_grad.astype(jnp.bfloat16), "dp", scatter_dimension=0, tiled=True
        ).astype(jnp.float32),
        lax.psum_scatter(
            out_grad.astype(jnp.bfloat16), "dp", scatter_dimension=0, tiled=True
        ).astype(jnp.float32),
        lax.psum_scatter(
            feed_part.astype(jnp.bfloat16), "dp", scatter_dimension=0, tiled=True
        ).astype(jnp.float32),
        lax.psum_scatter(
            gate_grad.astype(jnp.bfloat16), "dp", scatter_dimension=0, tiled=True
        ).astype(jnp.float32),
        lax.psum_scatter(
            up_grad.astype(jnp.bfloat16), "dp", scatter_dimension=0, tiled=True
        ).astype(jnp.float32),
        lax.psum_scatter(
            down_grad.astype(jnp.bfloat16), "dp", scatter_dimension=0, tiled=True
        ).astype(jnp.float32),
    )
    reduced = every_grad[:8] + (head_gain_grad,) + every_grad[8:]
    return (
        output,
        input_grad,
        reduced[0],
        reduced[1],
        reduced[2],
        reduced[3],
        reduced[4],
        reduced[5],
        reduced[6],
        reduced[7],
        reduced[8],
        reduced[9],
        reduced[10],
        reduced[11],
        reduced[12],
        reduced[13],
    )


def solution(mesh):
    placed = (
        P("dp", None),
        P("dp", None),
        P(),
        P("col", "row"),
        P("col", "row"),
        P("col", "row"),
        P("col", "row"),
        P(("row", "col"), None),
        P(("row", "col"), None),
        P(("row", "col"), None),
        P(),
        P("row", "col"),
        P(),
        P("col", "row"),
        P("col", "row"),
        P("row", "col"),
        P("dp", None),
    )
    return jax.shard_map(
        body,
        mesh=mesh,
        in_specs=placed,
        out_specs=(
            P("dp", None),
            P("dp", None),
            P("dp"),
            P(("col", "dp"), "row"),
            P(("col", "dp"), "row"),
            P(("col", "dp"), "row"),
            P(("col", "dp"), "row"),
            P(("row", "col", "dp"), None),
            P(("row", "col", "dp"), None),
            P(("row", "col", "dp"), None),
            P(),
            P(("row", "dp"), "col"),
            P("dp"),
            P(("col", "dp"), "row"),
            P(("col", "dp"), "row"),
            P(("row", "dp"), "col"),
        ),
        check_vma=False,
    )
```

profile of v0, /device:TPU:0, one launch (start us, length us, event | category | flops | bytes accessed | tf_op | source)
XLA Modules:
  0.0 1970.0 jit_solution(3801119176042480821)
XLA Ops:
  85.0 375.9 %while.38 = (s32[]{:T(128)}, f32[2,128,128]{2,1,0:T(8,128)S(1)}, f32[16,64,2,128]{3,1,2,0:T(8,128)}, f32[16,2,128,128]{3,2,1,0:T(8,128)}, s32[16,64]{1,0:T(8,128...) while((s32[]{:T(128)}, f32[2,128,128]{2,1,0:T(8,128)S(1)}, ...), condition=%wide.region_7.9_spmd.clone, body=%wide.region_6.8_spmd.clone.sunk | while | flops 126206208 | bytes 2016686 | solution.py:81
  89.5 9.8 custom-call.23
  113.0 9.8 custom-call.23
  136.5 9.8 custom-call.23
  160.0 9.8 custom-call.23
  183.5 9.8 custom-call.23
  206.9 9.8 custom-call.23
  230.4 9.8 custom-call.23
  253.9 9.8 custom-call.23
  277.4 9.8 custom-call.23
  300.9 9.8 custom-call.23
  324.4 9.8 custom-call.23
  347.9 9.8 custom-call.23
  371.4 9.8 custom-call.23
  394.9 9.8 custom-call.23
  418.4 9.8 custom-call.23
  441.9 9.8 custom-call.23
  470.3 10.3 all-gather.12.cloned.1.call-done
  485.5 105.2 %all-reduce.41.cloned.1.call-done = f32[1024,1024]{1,0:T(8,128)} async-done(((f32[1024,1024]{1,0:T(8,128)}), f32[1024,1024]{1,0:T(8,128)}) %all-reduce.41.cloned.1.call-update) | async-done | bytes 4194320 | tf_op jit(solution)/shard_map/psum | solution.py:138
  591.2 8.8 fusion.110
  600.1 11.9 all-gather.14.cloned.1.call-done
  617.9 8.6 broadcast_multiply_fusion
  640.2 9.4 pad_maximum_fusion
  649.7 21.4 %reduce-scatter.32.cloned.1.call-done = f32[512,2816]{1,0:T(8,128)} async-done(((f32[1024,2816]{1,0:T(8,128)}), f32[512,2816]{1,0:T(8,128)}) %reduce-scatter.32.cloned.1.call-update) | async-done | bytes 5767184 | tf_op jit(solution)/shard_map/reduce_scatter | solution.py:143
  678.3 17.4 all-gather.20.cloned.1.call-done
  706.1 105.2 %all-reduce.43.cloned.1.call-done = f32[1024,1024]{1,0:T(8,128)} async-done(((f32[1024,1024]{1,0:T(8,128)}), f32[1024,1024]{1,0:T(8,128)}) %all-reduce.43.cloned.1.call-update) | async-done | bytes 4194320 | tf_op jit(solution)/shard_map/psum | solution.py:138
  811.4 21.4 %all-gather.22.cloned.1.call-done = f32[1024,2048]{1,0:T(8,128)} async-done(((f32[1024,1024]{1,0:T(8,128)}), f32[1024,2048]{1,0:T(8,128)}) %all-gather.22.cloned.1.call-update) | async-done | bytes 8388624 | tf_op jit(solution)/shard_map/all_gather | solution.py:139
  832.7 10.7 multiply_reduce_fusion.2
  844.6 7.5 fusion.89
  858.7 8.9 reduce-scatter.36.cloned.1.call-done
  874.1 420.0 %while.39 = (s32[]{:T(128)}, f32[2,128,128]{2,1,0:T(8,128)S(1)}, f32[16,64,2,128]{3,2,1,0:T(2,128)}, f32[16,64,2,128]{3,1,2,0:T(8,128)S(1)}, f32[16,64,2,128]{3,...) while((s32[]{:T(128)}, f32[2,128,128]{2,1,0:T(8,128)S(1)}, ...), condition=%wide.region_21.23_spmd.clone, body=%wide.region_18.22_spmd.clone.sunk | while | flops 321499264 | bytes 6184963 | solution.py:81
  880.8 9.8 custom-call.24
  907.1 9.8 custom-call.24
  933.3 9.8 custom-call.24
  959.6 9.8 custom-call.24
  985.8 9.8 custom-call.24
  1012.1 9.8 custom-call.24
  1038.3 9.8 custom-call.24
  1064.6 9.8 custom-call.24
  1090.8 9.8 custom-call.24
  1117.1 9.8 custom-call.24
  1143.3 9.8 custom-call.24
  1169.6 9.8 custom-call.24
  1195.8 9.8 custom-call.24
  1222.1 9.8 custom-call.24
  1248.3 9.8 custom-call.24
  1274.6 9.8 custom-call.24
  1323.2 8.5 fusion.162
  1343.9 7.7 all-gather.28.cloned.1.call-done
  1358.3 7.6 convolution_convert_fusion
  1399.7 132.6 %all-reduce.45.cloned.1.call-done = (f32[1024,1024]{1,0:T(8,128)}, f32[1024,1024]{1,0:T(8,128)}) async-done(((f32[1024,1024]{1,0:T(8,128)}, f32[1024,1024]{1,0:T(8,128)}), (f32[1024,1024]{1,0:T(8,128)}, f32[1024,1024]{1,0:T(8,128)})) %all-reduce.45.cloned.1.call-update) | async-done | bytes 8388624 | tf_op jit(solution)/shard_map/psum | solution.py:138
  1534.3 57.0 %reduce-scatter.50.cloned.1.call-done = bf16[352,1024]{1,0:T(8,128)(2,1)} async-done(((bf16[1408,1024]{1,0:T(8,128)(2,1)}), bf16[352,1024]{1,0:T(8,128)(2,1)}) %reduce-scatter.50.cloned.1.call-update) | async-done | bytes 720912 | tf_op jit(solution)/shard_map/reduce_scatter | solution.py:320
  1593.7 56.0 %reduce-scatter.46.cloned.1.call-done = bf16[256,1408]{1,0:T(8,128)(2,1)} async-done(((bf16[1024,1408]{1,0:T(8,128)(2,1)}), bf16[256,1408]{1,0:T(8,128)(2,1)}) %reduce-scatter.46.cloned.1.call-update) | async-done | bytes 720912 | tf_op jit(solution)/shard_map/reduce_scatter | solution.py:314
  1652.0 55.9 %reduce-scatter.48.cloned.1.call-done = bf16[256,1408]{1,0:T(8,128)(2,1)} async-done(((bf16[1024,1408]{1,0:T(8,128)(2,1)}), bf16[256,1408]{1,0:T(8,128)(2,1)}) %reduce-scatter.48.cloned.1.call-update) | async-done | bytes 720912 | tf_op jit(solution)/shard_map/reduce_scatter | solution.py:317
  1710.2 27.0 %reduce-scatter.44.cloned.1.call-done = bf16[128,1024]{1,0:T(8,128)(2,1)} async-done(((bf16[512,1024]{1,0:T(8,128)(2,1)}), bf16[128,1024]{1,0:T(8,128)(2,1)}) %reduce-scatter.44.cloned.1.call-update) | async-done | bytes 262160 | tf_op jit(solution)/shard_map/reduce_scatter | solution.py:308
  1739.3 38.9 %psum.39 = f32[128]{0:T(128)} all-reduce(f32[128]{0:T(128)S(1)} %bitcast_reduce_fusion), channel_id=1, replica_groups=mesh['dp'=4,'row'=4,'col'=2] {'dp','row','col'}, use_global_device_ids=true, to_apply=%region_48.50 | all-reduce | flops 128 | bytes 1024 | tf_op jit(solution)/shard_map/psum | solution.py:282
  1781.0 16.4 reduce-scatter.54.cloned.1.call-done
  1798.7 19.3 reduce-scatter.52.cloned.1.call-done
  1819.5 26.2 %reduce-scatter.40.cloned.1.call-done = bf16[256,512]{1,0:T(8,128)(2,1)} async-done(((bf16[1024,512]{1,0:T(8,128)(2,1)}), bf16[256,512]{1,0:T(8,128)(2,1)}) %reduce-scatter.40.cloned.1.call-update) | async-done | bytes 262160 | tf_op jit(solution)/shard_map/reduce_scatter | solution.py:290
  1847.5 26.2 %reduce-scatter.38.cloned.1.call-done = bf16[256,512]{1,0:T(8,128)(2,1)} async-done(((bf16[1024,512]{1,0:T(8,128)(2,1)}), bf16[256,512]{1,0:T(8,128)(2,1)}) %reduce-scatter.38.cloned.1.call-update) | async-done | bytes 262160 | tf_op jit(solution)/shard_map/reduce_scatter | solution.py:287
  1875.4 26.4 %reduce-scatter.42.cloned.1.call-done = bf16[256,512]{1,0:T(8,128)(2,1)} async-done(((bf16[1024,512]{1,0:T(8,128)(2,1)}), bf16[256,512]{1,0:T(8,128)(2,1)}) %reduce-scatter.42.cloned.1.call-update) | async-done | bytes 262160 | tf_op jit(solution)/shard_map/reduce_scatter | solution.py:293
  1903.7 18.3 all-gather.30.cloned.1.call-done
  1928.1 12.1 all-reduce.36
  1944.4 18.3 fusion.91
  (1269 shorter events, 732.3 us)
Async XLA Ops:
  7.2 627.9 %copy-start = (bf16[1024,1408]{1,0:T(8,128)(2,1)S(1)}, bf16[1024,1408]{1,0:T(8,128)(2,1)}, u32[]{:S(2)}) copy-start(bf16[1024,1408]{1,0:T(8,128)(2,1)} %param.37) | copy-start | bytes 8650756
  7.2 36.1 %reduce-scatter.26.cloned.1.call-start = ((), (), s32[]{:S(2)}) async-start(), calls=%async_computation.17 | async-start | bytes 3145728 | tf_op jit(solution)/shard_map/reduce_scatter | solution.py:188
  22.4 33.5 %reduce-scatter.30.cloned.1.call-start = ((), (), s32[]{:S(2)}) async-start(), calls=%async_computation.19 | async-start | bytes 3145728 | tf_op jit(solution)/shard_map/reduce_scatter | solution.py:187
  26.9 34.1 %reduce-scatter.28.cloned.1.call-start = ((), (), s32[]{:S(2)}) async-start(), calls=%async_computation.18 | async-start | bytes 3145728 | tf_op jit(solution)/shard_map/reduce_scatter | solution.py:189
  31.4 11.0 copy-start.70
  31.4 11.6 copy-start.67
  31.4 11.7 copy-start.68
  31.4 11.7 copy-start.69
  31.5 449.1 %all-gather.12.cloned.1.call-start = ((), (), s32[]{:S(2)}) async-start(), calls=%async_computation.20 | async-start | bytes 1572864 | tf_op jit(solution)/shard_map/all_gather | solution.py:211
  39.0 11.4 copy-start.27
  43.0 18.0 copy-start.37
  43.0 18.0 copy-start.39
  43.1 18.0 copy-start.41
  43.1 18.0 copy-start.43
  43.1 18.0 copy-start.47
  43.1 18.0 copy-start.53
  43.1 18.0 copy-start.57
  43.2 17.9 copy-start.45
  43.2 17.9 copy-start.49
  43.2 17.9 copy-start.55
  43.2 17.9 copy-start.59
  470.3 120.4 %all-reduce.41.cloned.1.call-start = ((), (), s32[]{:S(2)}) async-start(), calls=%async_computation.21 | async-start | bytes 8388608 | tf_op jit(solution)/shard_map/psum | solution.py:138
  485.4 126.5 %all-gather.14.cloned.1.call-start = ((), (), s32[]{:S(2)}) async-start(), calls=%async_computation.22 | async-start | bytes 12582912 | tf_op jit(solution)/shard_map/all_gather | solution.py:139
  590.7 59.1 %reduce-scatter.34.cloned.1.call-start = ((), (), s32[]{:S(2)}) async-start(), calls=%async_computation.26 | async-start | bytes 8650752 | tf_op jit(solution)/shard_map/reduce_scatter | solution.py:143
  600.0 71.1 %reduce-scatter.32.cloned.1.call-start = ((), (), s32[]{:S(2)}) async-start(), calls=%async_computation.23 | async-start | bytes 17301504 | tf_op jit(solution)/shard_map/reduce_scatter | solution.py:143
  617.9 8.6 dynamic-slice-start
  649.7 46.0 %all-gather.20.cloned.1.call-start = ((), (), s32[]{:S(2)}) async-start(), calls=%async_computation.27 | async-start | bytes 8650752 | tf_op jit(solution)/shard_map/all_gather | solution.py:152
  678.2 133.0 %all-reduce.43.cloned.1.call-start = ((), (), s32[]{:S(2)}) async-start(), calls=%async_computation.28 | async-start | bytes 8388608 | tf_op jit(solution)/shard_map/psum | solution.py:138
  706.1 126.7 %copy-start.31 = (f32[2048]{0:T(1024)S(1)}, f32[2048]{0:T(1024)}, u32[]{:S(2)}) copy-start(f32[2048]{0:T(1024)} %param.35) | copy-start | bytes 24580
  706.1 126.6 %all-gather.22.cloned.1.call-start = ((), (), s32[]{:S(2)}) async-start(), calls=%async_computation.29 | async-start | bytes 12582912 | tf_op jit(solution)/shard_map/all_gather | solution.py:139
  811.3 56.3 %reduce-scatter.36.cloned.1.call-start = ((), (), s32[]{:S(2)}) async-start(), calls=%async_computation.30 | async-start | bytes 1572864 | tf_op jit(solution)/shard_map/reduce_scatter | solution.py:248
  832.7 10.8 copy-start.4
  832.7 11.9 copy-start.22
  844.6 10.8 copy-start.77
  855.4 13.8 copy-start.8
  855.4 13.8 copy-start.71
  857.8 465.4 %all-gather.16.cloned.1.call-start = ((), (), s32[]{:S(2)}) async-start(), calls=%async_computation.24 | async-start | bytes 4325376 | tf_op jit(solution)/shard_map/all_gather | solution.py:152
  858.5 475.1 %all-gather.26.cloned.1.call-start = ((), (), s32[]{:S(2)}) async-start(), calls=%async_computation.32 | async-start | bytes 1572864 | tf_op jit(solution)/shard_map/all_gather | solution.py:266
  1316.8 22.6 %all-gather.24.cloned.1.call-start = ((), (), s32[]{:S(2)}) async-start(), calls=%async_computation.31 | async-start | bytes 1572864 | tf_op jit(solution)/shard_map/all_gather | solution.py:265
  1319.9 31.8 %all-gather.28.cloned.1.call-start = ((), (), s32[]{:S(2)}) async-start(), calls=%async_computation.33 | async-start | bytes 1572864 | tf_op jit(solution)/shard_map/all_gather | solution.py:267
  1323.1 8.7 copy-start.28
  1323.1 10.5 copy-start.79
  1323.1 209.1 %all-reduce.45.cloned.1.call-start = ((), (), s32[]{:S(2)}) async-start(), calls=%async_computation.46 | async-start | bytes 16777216 | tf_op jit(solution)/shard_map/psum | solution.py:138
  1338.2 13.5 copy-start.81
  1358.3 233.0 %reduce-scatter.50.cloned.1.call-start = ((), (), s32[]{:S(2)}) async-start(), calls=%async_computation.41 | async-start | bytes 3604480 | tf_op jit(solution)/shard_map/reduce_scatter | solution.py:320
  1366.0 283.7 %reduce-scatter.46.cloned.1.call-start = ((), (), s32[]{:S(2)}) async-start(), calls=%async_computation.39 | async-start | bytes 3604480 | tf_op jit(solution)/shard_map/reduce_scatter | solution.py:314
  1372.7 335.2 %reduce-scatter.48.cloned.1.call-start = ((), (), s32[]{:S(2)}) async-start(), calls=%async_computation.40 | async-start | bytes 3604480 | tf_op jit(solution)/shard_map/reduce_scatter | solution.py:317
  1379.4 357.8 %reduce-scatter.44.cloned.1.call-start = ((), (), s32[]{:S(2)}) async-start(), calls=%async_computation.38 | async-start | bytes 1310720 | tf_op jit(solution)/shard_map/reduce_scatter | solution.py:308
  1385.1 393.1 %reduce-scatter.58.cloned.1.call-start = ((), (), s32[]{:S(2)}) async-start(), calls=%async_computation.45 | async-start | bytes 81920
  1385.9 393.7 %reduce-scatter.56.cloned.1.call-start = ((), (), s32[]{:S(2)}) async-start(), calls=%async_computation.44 | async-start | bytes 81920
  1386.8 410.6 %reduce-scatter.54.cloned.1.call-start = ((), (), s32[]{:S(2)}) async-start(), calls=%async_computation.43 | async-start | bytes 81920
  1387.6 430.4 %reduce-scatter.52.cloned.1.call-start = ((), (), s32[]{:S(2)}) async-start(), calls=%async_computation.42 | async-start | bytes 327680
  1389.0 456.7 %reduce-scatter.40.cloned.1.call-start = ((), (), s32[]{:S(2)}) async-start(), calls=%async_computation.36 | async-start | bytes 1310720 | tf_op jit(solution)/shard_map/reduce_scatter | solution.py:290
  1392.5 481.1 %reduce-scatter.38.cloned.1.call-start = ((), (), s32[]{:S(2)}) async-start(), calls=%async_computation.35 | async-start | bytes 1310720 | tf_op jit(solution)/shard_map/reduce_scatter | solution.py:287
  1396.1 505.8 %reduce-scatter.42.cloned.1.call-start = ((), (), s32[]{:S(2)}) async-start(), calls=%async_computation.37 | async-start | bytes 1310720 | tf_op jit(solution)/shard_map/reduce_scatter | solution.py:293
  1399.6 522.3 %all-gather.30.cloned.1.call-start = ((), (), s32[]{:S(2)}) async-start(), calls=%async_computation.34 | async-start | bytes 12582912 | tf_op jit(solution)/shard_map/all_gather | solution.py:139
  1532.3 412.1 %all-gather.18.cloned.1.call-start = ((), (), s32[]{:S(2)}) async-start(), calls=%async_computation.25 | async-start | bytes 12582912 | tf_op jit(solution)/shard_map/all_gather | solution.py:139
  1532.9 206.1 %copy-start.15 = (f32[16,64,2,128]{3,2,1,0:T(2,128)S(1)}, f32[16,64,2,128]{3,2,1,0:T(2,128)}, u32[]{:S(2)}) copy-start(f32[16,64,2,128]{3,2,1,0:T(2,128)} %copy.232) | copy-start | bytes 3145732
  1532.9 206.1 %copy-start.17 = (f32[1024,2,128]{2,1,0:T(2,128)S(1)}, f32[1024,2,128]{2,1,0:T(2,128)}, u32[]{:S(2)}) copy-start(f32[1024,2,128]{2,1,0:T(2,128)} %copy-done.16) | copy-start | bytes 3145732
  1532.9 206.1 %copy-start.23 = (bf16[1024,256]{1,0:T(8,128)(2,1)S(1)}, bf16[1024,256]{1,0:T(8,128)(2,1)}, u32[]{:S(2)}) copy-start(bf16[1024,256]{1,0:T(8,128)(2,1)} %reduce-scatter.36.cloned.1.call-done) | copy-start | bytes 1572868
  1652.0 270.0 %copy-start.30 = (f32[1024]{0:T(1024)S(1)}, f32[1024]{0:T(1024)}, u32[]{:S(2)}) copy-start(f32[1024]{0:T(1024)} %copy-done.29) | copy-start | bytes 12292
  1652.0 270.0 %copy-start.33 = (f32[2048]{0:T(1024)S(1)}, f32[2048]{0:T(1024)}, u32[]{:S(2)}) copy-start(f32[2048]{0:T(1024)} %param.25) | copy-start | bytes 24580
  1903.7 37.2 %copy-start.35 = (f32[1024]{0:T(1024)S(1)}, f32[1024]{0:T(1024)}, u32[]{:S(2)}) copy-start(f32[1024]{0:T(1024)} %copy-done.34) | copy-start | bytes 12292
  1944.4 18.3 copy-start.1
  (51 other events, 212.2 us)
Sparse Core Ops, SparseCore 0:
  22.5 12.3 reduce-scatter.25
  37.2 10.7 reduce-scatter.29
  50.2 10.7 reduce-scatter.27
  470.4 10.1 all-gather.11
  485.6 105.0 all-reduce.40
  592.1 19.8 all-gather.13
  614.2 14.9 reduce-scatter.33
  649.8 21.3 reduce-scatter.31
  678.4 17.2 all-gather.19
  706.2 105.0 all-reduce.42
  812.8 19.8 all-gather.21
  857.9 9.6 reduce-scatter.35
  869.8 12.8 all-gather.15
  1317.0 10.1 all-gather.25
  1329.2 10.1 all-gather.23
  1341.4 10.1 all-gather.27
  1358.4 173.8 all-reduce.44
  1534.4 56.8 reduce-scatter.49
  1593.6 56.0 reduce-scatter.45
  1651.8 56.0 reduce-scatter.47
  1710.2 26.9 reduce-scatter.43
  1739.6 17.6 reduce-scatter.57
  1760.1 17.2 reduce-scatter.55
  1780.1 17.1 reduce-scatter.53
  1800.2 17.7 reduce-scatter.51
  1820.2 25.3 reduce-scatter.39
  1847.8 25.7 reduce-scatter.37
  1876.0 25.7 reduce-scatter.41
  1903.4 18.4 all-gather.29
  1923.3 21.0 all-gather.17
where the time goes:
time: 1990 us; the launch traced here: 1970 us
  waiting for transfers between devices  782 us (39%)
  other arithmetic  534 us (27%)
  matrix products  338 us (17%)
  local copies, waits for them, and re-layouts  235 us (12%)
  blocking collectives  56.6 us (3%)
    psum x3, waiting for transfers between devices, grid_total(): summed = lax.psum(partial_value, 'row')  343 us
    another operation x80, other arithmetic, span_step(): lax.linalg.triangular_solve(system, target, left_side=True, lower=True)  316 us
    squeeze x112, local copies, waits for them, and re-layouts, delta_rule(): lax.scan(jax.checkpoint(span_step), start_memory, (queries.reshape(blocks...  90.8 us
    reduce_scatter x1, waiting for transfers between devices, body(): lax.psum_scatter(down_grad.astype(jnp.bfloat16), 'dp', scatter_dimension=...  57 us
    reduce_scatter x1, waiting for transfers between devices, body(): lax.psum_scatter(gate_grad.astype(jnp.bfloat16), 'dp', scatter_dimension=...  56 us
    reduce_scatter x1, waiting for transfers between devices, body(): lax.psum_scatter(up_grad.astype(jnp.bfloat16), 'dp', scatter_dimension=0,...  55.9 us
    all_gather x4, waiting for transfers between devices, grid_total(): return lax.all_gather(summed, 'col', axis=1, tiled=True)  55 us
    dot_general x48, matrix products, span_step(): jnp.einsum('hcv,hck->hvk', writes * closing[None, :, None], key_heads, pr...  41.5 us
  transfers between devices with their start and end apart: 30, of which 23 were waited for; matrix products, arithmetic and copies ran while one was open for 31% of the time, Pallas kernels for 0%

commit v1 on v0

v1 whole, which is shorter than its diff:
```python
import functools
import jax
import jax.numpy as jnp
from jax import lax
from jax.experimental import pallas as pl
from jax.experimental.pallas import tpu as pltpu
from jax.sharding import PartitionSpec as P

EPSILON = 1e-06
HEAD_FLOOR = 0.02
CH = 128
HS = 128
F32 = jnp.float32
BF16 = jnp.bfloat16

NN = (((1,), (0,)), ((), ()))
NT = (((1,), (1,)), ((), ()))
TN = (((0,), (0,)), ((), ()))


def dot1(a, b, dims=NN):
    return lax.dot_general(a.astype(BF16), b.astype(BF16), dims, preferred_element_type=F32)


def split(a):
    hi = a.astype(BF16)
    return hi, (a - hi.astype(F32)).astype(BF16)


def dot3s(a, b, dims=NN):
    (ah, al), (bh, bl) = a, b
    d = functools.partial(lax.dot_general, dimension_numbers=dims, preferred_element_type=F32)
    return d(ah, bh) + (d(ah, bl) + d(al, bh))


def dot3(a, b, dims=NN):
    return dot3s(split(a), split(b), dims)


def silu_parts(z):
    s = 1.0 / (1.0 + jnp.exp(-z))
    return s, z * s


def unit_inverse(low, xor, eye, dot):
    inv = eye - jnp.where(xor < 2, low, 0.0)
    size = 2
    while size < CH:
        part = jnp.where((xor >= size) & (xor < 2 * size), low, 0.0)
        inv = inv - dot(dot(inv, part), inv)
        size *= 2
    return inv


def window(ref, c, cols):
    return ref[pl.ds(pl.multiple_of(c * CH, CH), CH + 8), cols]


def conv_chunk(win, taps, masks):
    out = win[8:] * taps[3]
    for j in (1, 2, 3):
        out = out + masks[j - 1] * pltpu.roll(win, j, 0)[8:] * taps[3 - j]
    return out


def chunk_docs(doc_col, doc_row, c):
    col = doc_col[pl.ds(pl.multiple_of(c * CH + 8, 8), CH), :]
    row = doc_row[pl.ds(c, 1), :]
    prev = doc_col[pl.ds(pl.multiple_of(c * CH, 8), 8), :][7:8]
    last = col[CH - 1:CH]
    return col, row, prev, last


def place_rows(place, c):
    return pl.ds(pl.multiple_of(place[c] * CH, CH), CH)


def fill_pad(pad, place, z_ref, chunks, width):
    pad[0:8] = jnp.zeros((8, 3 * width), F32)
    for c in range(chunks):
        pad[c * CH + 8:(c + 1) * CH + 8] = z_ref[place_rows(place, c), :3 * width]


def fwd_kernel(heads, chunks, dotg, doti, dot,
               place, z_ref, taps_ref, doc_col, doc_row, gain_ref,
               out_ref, mixed_ref, t_ref, h_ref, a_ref, qt_ref, w_ref, u_ref,
               pad, pu_s, b_s):
    width = heads * HS
    fill_pad(pad, place, z_ref, chunks, width)
    row_i = lax.broadcasted_iota(jnp.int32, (CH, CH), 0)
    col_i = lax.broadcasted_iota(jnp.int32, (CH, CH), 1)
    xor = row_i ^ col_i
    eye = (xor == 0).astype(F32)

    def one(c, h):
        col, row, prev, last = chunk_docs(doc_col, doc_row, c)
        same = col == row
        strict = same & (row_i > col_i)
        incl = same & (row_i >= col_i)
        carried = (col == prev).astype(F32)
        closing = (col == last).astype(F32)
        keep = (last == prev).astype(F32)
        dwin = doc_col[pl.ds(pl.multiple_of(c * CH, CH), CH + 8), :]
        masks = [(dwin[8 - j:CH + 8 - j] == col).astype(F32) for j in (1, 2, 3)]

        def conv(which):
            cols = slice(which * width + h * HS, which * width + (h + 1) * HS)
            taps = [taps_ref[t:t + 1, cols] for t in range(4)]
            return silu_parts(conv_chunk(window(pad, c, cols), taps, masks))[1]

        q, k, v = conv(0), conv(1), conv(2)
        k = k * lax.rsqrt(jnp.sum(k * k, axis=1, keepdims=True) + EPSILON)
        beta = 1.0 / (1.0 + jnp.exp(-z_ref[place_rows(place, c), 3 * width + h:3 * width + h + 1]))
        gram = dotg(k, k, NT)
        low = jnp.where(strict, beta * gram, 0.0)
        inv = unit_inverse(low, xor, eye, doti)
        w = dot(inv, (carried * beta) * k)
        u = dot(inv, beta * v)
        p = jnp.where(incl, dot(q, k, NT), 0.0)
        qt = carried * q - dot(p, w)
        pu = dot(p, u)
        kcl = closing * k
        a = keep * eye - dot(kcl, w, TN)
        b = dot(kcl, u, TN)
        i = c * heads + h
        t_ref[i] = inv
        qt_ref[i] = qt
        a_ref[i] = a
        w_ref[i] = w
        u_ref[i] = u
        pu_s[i] = pu
        b_s[i] = b

    per = 2

    def phase_one(g, carry):
        for e in range(per):
            for h in range(heads):
                one(g * per + e, h)
        return carry

    lax.fori_loop(0, chunks // per, phase_one, 0)

    def phase_two(c, state):
        new = []
        for h in range(heads):
            i = c * heads + h
            h_ref[i] = state[h]
            new.append(dot(a_ref[i], state[h]) + b_s[i])
        return tuple(new)

    lax.fori_loop(0, chunks, phase_two, tuple(jnp.zeros((HS, HS), F32) for _ in range(heads)))

    def phase_three(c, carry):
        for h in range(heads):
            i = c * heads + h
            rows = pl.ds(pl.multiple_of(c * CH, CH), CH)
            cols = slice(h * HS, (h + 1) * HS)
            mixed = dot(qt_ref[i], h_ref[i]) + pu_s[i]
            mixed_ref[rows, cols] = mixed
            r = lax.rsqrt(jnp.mean(mixed * mixed, axis=1, keepdims=True) + HEAD_FLOOR)
            out_ref[place_rows(place, c), cols] = (mixed * r * gain_ref[...]).astype(BF16)
        return carry

    lax.fori_loop(0, chunks, phase_three, 0)


def vm(n):
    return [pl.BlockSpec(memory_space=pltpu.VMEM)] * n


SMEM = pl.BlockSpec(memory_space=pltpu.SMEM)


def delta_forward(place, z, taps, doc_col, doc_row, gain, dots=(dot3, dot3, dot3)):
    tokens, width = z.shape[0], taps.shape[1] // 3
    heads = width // HS
    chunks = tokens // CH
    n = chunks * heads
    sq = jax.ShapeDtypeStruct((n, CH, HS), F32)
    return pl.pallas_call(
        functools.partial(fwd_kernel, heads, chunks, *dots),
        out_shape=(jax.ShapeDtypeStruct((tokens, width), BF16), jax.ShapeDtypeStruct((tokens, width), F32),
                   sq, sq, sq, sq, sq, sq),
        in_specs=[SMEM] + vm(5), out_specs=tuple(vm(8)),
        scratch_shapes=[pltpu.VMEM((tokens + 8, 3 * width), F32), pltpu.VMEM((n, CH, HS), F32), pltpu.VMEM((n, CH, HS), F32)],
        compiler_params=pltpu.CompilerParams(vmem_limit_bytes=48 * 1024 * 1024),
        cost_estimate=pl.CostEstimate(flops=60_000_000_000, bytes_accessed=16_000_000, transcendentals=0),
        name="delta_forward",
    )(place, z, taps, doc_col, doc_row, gain)


def bwd_kernel(heads, chunks, dotg, dot,
               place, dh_ref, z_ref, taps_ref, doc_col, doc_row, gain_ref,
               mixed_ref, t_ref, h_ref, a_ref, qt_ref, w_ref, u_ref,
               dz_ref, dtaps_ref, dgain_ref,
               pad, do_s, eb_s, e_s, dc_s):
    width = heads * HS
    tokens = chunks * CH
    fill_pad(pad, place, z_ref, chunks, width)
    dz_ref[:, 3 * width:] = jnp.zeros((tokens, dz_ref.shape[1] - 3 * width), BF16)
    dc_s[tokens:] = jnp.zeros((8, 3 * width), F32)
    dtaps_ref[...] = jnp.zeros_like(dtaps_ref)
    row_i = lax.broadcasted_iota(jnp.int32, (CH, CH), 0)
    col_i = lax.broadcasted_iota(jnp.int32, (CH, CH), 1)

    def rows_of(c):
        return pl.ds(pl.multiple_of(c * CH, CH), CH)

    def phase_one(c, total):
        for h in range(heads):
            i = c * heads + h
            cols = slice(h * HS, (h + 1) * HS)
            m = mixed_ref[rows_of(c), cols]
            dy = dh_ref[place_rows(place, c), cols].astype(F32)
            r = lax.rsqrt(jnp.mean(m * m, axis=1, keepdims=True) + HEAD_FLOOR)
            mr = m * r
            total = total + jnp.sum(dy * mr, axis=0, keepdims=True)
            gy = gain_ref[...] * dy
            dm = r * (gy - mr * jnp.mean(mr * gy, axis=1, keepdims=True))
            do_s[i] = dm
            eb_s[i] = dot(qt_ref[i], dm, TN)
        return total

    dgain_ref[...] = lax.fori_loop(0, chunks, phase_one, jnp.zeros((1, HS), F32))

    def phase_two(n, state):
        c = chunks - 1 - n
        new = []
        for h in range(heads):
            i = c * heads + h
            e_s[i] = state[h]
            new.append(dot(a_ref[i], state[h], TN) + eb_s[i])
        return tuple(new)

    lax.fori_loop(0, chunks, phase_two, tuple(jnp.zeros((HS, HS), F32) for _ in range(heads)))

    def one(c, h):
        i = c * heads + h
        col, row, prev, last = chunk_docs(doc_col, doc_row, c)
        same = col == row
        strict = same & (row_i > col_i)
        incl = same & (row_i >= col_i)
        carried = (col == prev).astype(F32)
        closing = (col == last).astype(F32)
        dwin = doc_col[pl.ds(pl.multiple_of(c * CH, CH), CH + 8), :]
        masks = [(dwin[8 - j:CH + 8 - j] == col).astype(F32) for j in (1, 2, 3)]

        def conv(which):
            cols = slice(which * width + h * HS, which * width + (h + 1) * HS)
            taps = [taps_ref[t:t + 1, cols] for t in range(4)]
            z = conv_chunk(window(pad, c, cols), taps, masks)
            s, y = silu_parts(z)
            return y, s + y * (1.0 - s)

        q, q_slope = conv(0)
        k, k_slope = conv(1)
        v, v_slope = conv(2)
        n = lax.rsqrt(jnp.sum(k * k, axis=1, keepdims=True) + EPSILON)
        k = k * n
        beta = 1.0 / (1.0 + jnp.exp(-z_ref[place_rows(place, c), 3 * width + h:3 * width + h + 1]))
        inv, state, w, u, dm, e = t_ref[i], h_ref[i], w_ref[i], u_ref[i], do_s[i], e_s[i]
        gram = dotg(k, k, NT)
        p = jnp.where(incl, dot(q, k, NT), 0.0)
        r = u - dot(w, state)
        y = v - carried * dot(k, state)
        dr = dot(p, dm, TN) + closing * dot(k, e)
        x = dot(inv, dr, TN)
        dp = jnp.where(incl, dot(dm, r, NT), 0.0)
        dq = dot(dp, k) + carried * dot(dm, state, NT)
        dlow = jnp.where(strict, -dot(x, r, NT), 0.0)
        dgram = beta * dlow
        dk = closing * dot(r, e, NT) + dot(dp, q, TN) + dot(dgram, k) + dot(dgram, k, TN) - (carried * beta) * dot(x, state, NT)
        dbeta = jnp.sum(dlow * gram, axis=1, keepdims=True) + jnp.sum(x * y, axis=1, keepdims=True)
        dk = n * (dk - k * jnp.sum(k * dk, axis=1, keepdims=True))
        for which, value in ((0, dq * q_slope), (1, dk * k_slope), (2, beta * x * v_slope)):
            dc_s[rows_of(c), which * width + h * HS:which * width + (h + 1) * HS] = value
        dz_ref[place_rows(place, c), 3 * width + h:3 * width + h + 1] = (dbeta * beta * (1.0 - beta)).astype(BF16)

    per = 2

    def phase_three(g, carry):
        for e in range(per):
            for h in range(heads):
                one(g * per + e, h)
        return carry

    lax.fori_loop(0, chunks // per, phase_three, 0)

    def phase_four(c, carry):
        dwin = doc_col[pl.ds(pl.multiple_of(c * CH, CH), CH + 8), :]
        col = dwin[8:]
        after = doc_col[pl.ds(pl.multiple_of(c * CH + 8, 8), CH + 8), :]
        masks = [(dwin[8 - j:CH + 8 - j] == col).astype(F32) for j in (1, 2, 3)]
        later = [(after[j:CH + j] == col).astype(F32) for j in (1, 2, 3)]
        for b in range(3 * heads):
            cols = slice(b * HS, (b + 1) * HS)
            win = window(pad, c, cols)
            dwn = dc_s[pl.ds(pl.multiple_of(c * CH, CH), CH + 8), cols]
            d = dwn[:CH]
            dz = d * taps_ref[3:4, cols]
            dtaps_ref[3:4, cols] += jnp.sum(d * win[8:], axis=0, keepdims=True)
            for j in (1, 2, 3):
                dz = dz + later[j - 1] * pltpu.roll(dwn, CH + 8 - j, 0)[:CH] * taps_ref[3 - j:4 - j, cols]
                dtaps_ref[3 - j:4 - j, cols] += jnp.sum(masks[j - 1] * pltpu.roll(win, j, 0)[8:] * d, axis=0, keepdims=True)
            dz_ref[place_rows(place, c), cols] = dz.astype(BF16)
        return carry

    lax.fori_loop(0, chunks, phase_four, 0)


def delta_backward(place, dheads, z, taps, doc_col, doc_row, gain, saved, dots=(dot3, dot3)):
    tokens, width = z.shape[0], taps.shape[1] // 3
    heads = width // HS
    chunks = tokens // CH
    n = chunks * heads
    sq = pltpu.VMEM((n, CH, HS), F32)
    return pl.pallas_call(
        functools.partial(bwd_kernel, heads, chunks, *dots),
        out_shape=(jax.ShapeDtypeStruct(z.shape, BF16), jax.ShapeDtypeStruct((4, 3 * width), F32),
                   jax.ShapeDtypeStruct((1, HS), F32)),
        in_specs=[SMEM] + vm(13), out_specs=tuple(vm(3)),
        scratch_shapes=[pltpu.VMEM((tokens + 8, 3 * width), F32), sq, sq, sq, pltpu.VMEM((tokens + 8, 3 * width), F32)],
        compiler_params=pltpu.CompilerParams(vmem_limit_bytes=48 * 1024 * 1024),
        cost_estimate=pl.CostEstimate(flops=50_000_000_000, bytes_accessed=16_000_000, transcendentals=0),
        name="delta_backward",
    )(place, dheads, z, taps, doc_col, doc_row, gain, *saved)


def norm_kernel(chunk_of, half_of, a_ref, b_ref, gain_ref, out_ref):
    half = a_ref.shape[1]
    a, b = a_ref[...].astype(F32), b_ref[...].astype(F32)
    total = jnp.sum(a * a, axis=1, keepdims=True) + jnp.sum(b * b, axis=1, keepdims=True)
    r = lax.rsqrt(total / (2 * half) + EPSILON)
    out_ref[:, :half] = (a * r * gain_ref[:, :half]).astype(BF16)
    out_ref[:, half:] = (b * r * gain_ref[:, half:]).astype(BF16)


def copy_kernel(chunk_of, half_of, a_ref, b_ref, out_ref):
    half = a_ref.shape[1]
    out_ref[:, :half] = a_ref[...]
    out_ref[:, half:] = b_ref[...]


def ordered(kernel, chunk_of, half_of, x, *rest):
    tokens, width = x.shape
    half = width // 2
    return pl.pallas_call(
        kernel,
        grid_spec=pltpu.PrefetchScalarGridSpec(
            num_scalar_prefetch=2,
            grid=(tokens // CH,),
            in_specs=[
                pl.BlockSpec((CH, half), lambda p, ch, hf: (ch[p], hf[0])),
                pl.BlockSpec((CH, half), lambda p, ch, hf: (ch[p], hf[1])),
            ] + [pl.BlockSpec((1, width), lambda p, ch, hf: (0, 0)) for _ in rest],
            out_specs=pl.BlockSpec((CH, width), lambda p, ch, hf: (p, 0)),
        ),
        out_shape=jax.ShapeDtypeStruct((tokens, width), BF16),
        compiler_params=pltpu.CompilerParams(vmem_limit_bytes=32 * 1024 * 1024),
        cost_estimate=pl.CostEstimate(flops=10 * tokens * width, bytes_accessed=4 * tokens * width, transcendentals=0),
        name="ordered_rows",
    )(chunk_of, half_of, x, x, *rest)


def place_kernel(count, chunk_of, half_of, *refs):
    out = refs[2 * count]
    half = out.shape[1] // 2
    for p in range(2 * count):

        @pl.when(pl.program_id(0) == p)
        def _(p=p):
            for h in range(2):
                to = half_of[h] if p < count else half_of[1 - h]
                out[:, pl.ds(pl.multiple_of(to * half, half), half)] = refs[p][:, h * half:(h + 1) * half]


def place(chunk_of, half_of, own, partner):
    count = len(own)
    rows, width = own[0].shape
    return pl.pallas_call(
        functools.partial(place_kernel, count),
        grid_spec=pltpu.PrefetchScalarGridSpec(
            num_scalar_prefetch=2,
            grid=(2 * count,),
            in_specs=[pl.BlockSpec((rows, width), lambda p, ch, hf: (0, 0)) for _ in range(2 * count)],
            out_specs=pl.BlockSpec((rows, width), lambda p, ch, hf: (ch[p], 0)),
        ),
        out_shape=jax.ShapeDtypeStruct((2 * count * rows, width), own[0].dtype),
        compiler_params=pltpu.CompilerParams(vmem_limit_bytes=32 * 1024 * 1024),
        cost_estimate=pl.CostEstimate(flops=0, bytes_accessed=8 * count * rows * width, transcendentals=0),
        name="place_rows",
    )(chunk_of, half_of, *own, *partner)


def mm(left, right, dims=NN):
    return lax.dot_general(left, right, dims, preferred_element_type=F32)


def body(
    inputs, segments, mixer_gain, w_query, w_key, w_value, w_beta, conv_query, conv_key, conv_value,
    head_gain, w_out, feed_gain, w_gate, w_up, w_down, cotangent,
):
    cols, rows, groups = lax.axis_size("col"), lax.axis_size("row"), lax.axis_size("dp")
    c, r, g = lax.axis_index("col"), lax.axis_index("row"), lax.axis_index("dp")
    tokens, width = inputs.shape
    half, mine = width // cols, tokens // cols
    own_width = conv_query.shape[0]
    own_heads = own_width // HS
    feed = w_gate.shape[1]

    def swap(v):
        return lax.ppermute(v, "col", [(i, i ^ 1) for i in range(cols)])

    def to_row(v, k):
        return lax.ppermute(v, "row", [(i, i ^ k) for i in range(rows)])

    def row_sum(blocks):
        total = blocks[0]
        for k in range(rows - 1, 0, -1):
            total = total + to_row(blocks[k], k).astype(F32)
        return total

    def row_gather(own):
        return [own] + [to_row(own, k) for k in range(1, rows)]

    def own_first(v, axis=-1):
        size = v.shape[axis] // 2
        return jnp.concatenate([lax.dynamic_slice_in_dim(v, i * size, size, axis) for i in (c, 1 - c)], axis)

    def group_sum(v, flip=0):
        step, shards = 1, groups
        v = v.astype(BF16)
        while step < groups:
            bit = (g // step) % 2
            if step * 2 == groups:
                bit = bit ^ flip
            parts = v.reshape(shards // 2, 2, -1, v.shape[-1])
            keep = lax.dynamic_index_in_dim(parts, bit, 1, keepdims=False)
            send = lax.dynamic_index_in_dim(parts, 1 - bit, 1, keepdims=False)
            got = lax.ppermute(send, "dp", [(i, i ^ step) for i in range(groups)])
            v = keep.astype(F32) + got.astype(F32)
            step, shards = step * 2, shards // 2
            v = v.reshape(-1, v.shape[-1])
            if step < groups:
                v = v.astype(BF16)
        return v

    def all_sum(v):
        v = v + swap(v)
        k = 1
        while k < rows:
            v = v + to_row(v, k)
            k *= 2
        k = 1
        while k < groups:
            v = v + lax.ppermute(v, "dp", [(i, i ^ k) for i in range(groups)])
            k *= 2
        return v

    order = jnp.arange(cols * rows, dtype=jnp.int32)
    chunk_of = ((order % rows) ^ r) * cols + ((order // rows) ^ c)
    place_of = ((order % cols) ^ c) * rows + ((order // cols) ^ r)
    half_of = jnp.stack([c, 1 - c]).astype(jnp.int32)
    documents = (segments + (jnp.arange(segments.shape[0], dtype=jnp.int32) * segments.shape[1])[:, None]).reshape(-1)
    doc_col = jnp.pad(documents, (8, 8), constant_values=-1)[:, None]
    doc_row = documents.reshape(-1, CH)
    taps = jnp.concatenate([conv_query.T, conv_key.T, conv_value.T], 1)
    gain_row = head_gain[None]
    gain_one, gain_two = own_first(mixer_gain)[None], own_first(feed_gain)[None]

    def columns(i):
        parts = [lax.dynamic_slice_in_dim(w, i * own_width, own_width, 1) for w in (w_query, w_key, w_value)]
        beta = lax.dynamic_slice_in_dim(w_beta, i * own_heads, own_heads, 1)
        return jnp.concatenate(parts + [jnp.pad(beta, ((0, 0), (0, HS - own_heads)))], 1)

    w_own, w_oth = columns(c), columns(1 - c)
    w_own_x = swap(w_oth)
    act = ordered(norm_kernel, chunk_of, half_of, inputs, gain_one)
    z = mm(act[:, :half], w_own) + mm(act[:, half:], w_own_x)
    heads, *saved = delta_forward(place_of, z, taps, doc_col, doc_row, gain_row)
    w_out_x, w_gate_x, w_up_x, w_down_x, w_oth_x = swap(w_out), swap(w_gate), swap(w_up), swap(w_down), swap(w_own)
    w_out_all = jnp.concatenate([own_first(w_out, 0), own_first(w_out_x, 0)], 1)

    heads_0 = jnp.concatenate([heads[:mine], swap(heads[mine:])], 1)
    away = mm(heads_0[CH:], w_out_all).astype(BF16)
    near = mm(heads_0[:CH], w_out_all)
    attended = row_sum([near] + [away[k * CH:(k + 1) * CH] for k in range(rows - 1)])
    cot = ordered(copy_kernel, chunk_of, half_of, cotangent)
    upstream = cot[:CH].astype(F32)
    d_hidden = mm(cot[:mine, :half], w_down, NT) + mm(cot[:mine, half:], w_down_x, NT)

    x_own = own_first(lax.dynamic_slice_in_dim(inputs, chunk_of[0] * CH, CH, 0)).astype(F32)
    middle = x_own + attended
    norm_two = lax.rsqrt(jnp.mean(middle * middle, axis=1, keepdims=True) + EPSILON)
    act_two = jnp.concatenate(row_gather((middle * norm_two * gain_two).astype(BF16)), 0)
    gate = mm(act_two[:, :half], w_gate) + mm(act_two[:, half:], w_gate_x)
    upward = mm(act_two[:, :half], w_up) + mm(act_two[:, half:], w_up_x)
    s = jax.nn.sigmoid(gate)
    hidden = (gate * s * upward).astype(BF16)
    d_gate = (d_hidden * upward * s * (1.0 + gate * (1.0 - s))).astype(BF16)
    d_up = (d_hidden * gate * s).astype(BF16)

    def back_two(a, b):
        return jnp.concatenate([mm(a, w_gate, NT) + mm(b, w_up, NT), mm(a, w_gate_x, NT) + mm(b, w_up_x, NT)], 1)

    away = back_two(d_gate[CH:], d_up[CH:]).astype(BF16)
    near = back_two(d_gate[:CH], d_up[:CH])
    d_act_two = row_sum([near] + [away[k * CH:(k + 1) * CH] for k in range(rows - 1)])

    def norm_back(values, inverse, gains, grads):
        scaled = gains * grads
        normal = values * inverse
        shift = jnp.mean(normal * scaled, axis=1, keepdims=True)
        return inverse * (scaled - normal * shift), jnp.sum(grads * normal, axis=0)

    d_norm, feed_part = norm_back(middle, norm_two, gain_two, d_act_two)
    d_middle = upstream + d_norm
    d_att = jnp.concatenate(row_gather(d_middle.astype(BF16)), 0)
    d_heads = mm(d_att, w_out_all, NT).astype(BF16)
    d_heads = jnp.concatenate([d_heads[:, :own_width], swap(d_heads[:, own_width:])], 0)
    dz, d_taps, head_part = delta_backward(place_of, d_heads, z, taps, doc_col, doc_row, gain_row, saved)

    act_two_x, hidden_x, d_gate_x, d_up_x = swap(act_two[:, half:]), swap(hidden), swap(d_gate), swap(d_up)
    cot_x = cot[mine:, :half]
    down_grad = mm(hidden, cot[:mine, :half], TN) + mm(hidden_x, cot_x, TN)
    gate_grad = mm(act_two[:, :half], d_gate, TN) + mm(act_two_x, d_gate_x, TN)
    up_grad = mm(act_two[:, :half], d_up, TN) + mm(act_two_x, d_up_x, TN)
    down_grad, gate_grad, up_grad = group_sum(down_grad), group_sum(gate_grad), group_sum(up_grad)
    heads_1 = jnp.concatenate([heads[mine:], swap(heads[:mine])], 1)
    out_grad = mm(heads_0, d_att[:, :half], TN) + mm(heads_1, swap(d_att[:, half:]), TN)
    out_grad = group_sum(out_grad, c)

    def feed_out(h):
        return jnp.concatenate([mm(h, w_down), mm(h, w_down_x)], 1)

    away = feed_out(hidden[CH:]).astype(BF16)
    near = feed_out(hidden[:CH])
    output = (middle + row_sum([near] + [away[k * CH:(k + 1) * CH] for k in range(rows - 1)])).astype(BF16)
    output = row_gather(output)
    output = place(chunk_of, half_of, output, [swap(v) for v in output])

    dz_0 = swap(dz[mine:])
    dz_1 = swap(dz[:mine])

    def back_one(a, b):
        return jnp.concatenate([mm(a, w_own, NT) + mm(b, w_oth, NT), mm(a, w_own_x, NT) + mm(b, w_oth_x, NT)], 1)

    away = back_one(dz[CH:mine], dz_0[CH:]).astype(BF16)
    near = back_one(dz[:CH], dz_0[:CH])
    d_act = row_sum([near] + [away[k * CH:(k + 1) * CH] for k in range(rows - 1)])
    norm_one = lax.rsqrt(jnp.mean(x_own * x_own, axis=1, keepdims=True) + EPSILON)
    d_norm, mixer_part = norm_back(x_own, norm_one, gain_one, d_act)
    input_grad = row_gather((d_middle + d_norm).astype(BF16))
    input_grad = place(chunk_of, half_of, input_grad, [swap(v) for v in input_grad])
    grad_own = mm(act[:, :half], dz, TN)
    grad_oth = mm(act[:, :half], jnp.concatenate([dz_0, dz_1], 0), TN)
    grads = group_sum(jnp.concatenate([grad_own, grad_oth], 1))
    span = grads.shape[1] // 2

    def projection(start, size):
        a, b = grads[:, start:start + size], grads[:, span + start:span + start + size]
        return jnp.where(c == 0, jnp.concatenate([a, b], 1), jnp.concatenate([b, a], 1))

    query_grad, key_grad, value_grad = (projection(i * own_width, own_width) for i in range(3))
    beta_grad = projection(3 * own_width, own_heads)

    small = all_sum(jnp.concatenate([own_first(mixer_part), own_first(feed_part), head_part[0]]).reshape(-1, HS)).reshape(-1)
    share = width // groups
    mixer_gain_grad = lax.dynamic_slice_in_dim(small, g * share, share)
    feed_gain_grad = lax.dynamic_slice_in_dim(small, width + g * share, share)
    head_gain_grad = small[2 * width:]
    k = 1
    while k < groups:
        d_taps = d_taps + lax.ppermute(d_taps, "dp", [(i, i ^ k) for i in range(groups)])
        k *= 2
    share = own_width // groups
    conv_grads = [
        lax.dynamic_slice_in_dim(d_taps, i * own_width + g * share, share, 1).T for i in range(3)
    ]
    return (
        output, input_grad, mixer_gain_grad, query_grad, key_grad, value_grad, beta_grad, *conv_grads,
        head_gain_grad, out_grad, feed_gain_grad, gate_grad, up_grad, down_grad,
    )


def solution(mesh):
    weight, swapped = P("col", "row"), P("row", "col")
    taps = P(("row", "col"), None)
    grad, grad_taps = P(("col", "dp"), "row"), P(("row", "col", "dp"), None)
    grad_swapped = P(("row", "dp"), "col")
    tokens = P("dp", None)
    return jax.shard_map(
        body,
        mesh=mesh,
        in_specs=(
            tokens, tokens, P(), weight, weight, weight, weight, taps, taps, taps, P(), swapped, P(), weight, weight,
            swapped, tokens,
        ),
        out_specs=(
            tokens, tokens, P("dp"), grad, grad, grad, grad, grad_taps, grad_taps, grad_taps, P(), grad_swapped, P("dp"),
            grad, grad, grad_swapped,
        ),
        check_vma=False,
    )
```

time: 1990 us -> 676 us (0.34)
  other arithmetic: 534 us -> 19.1 us
  waiting for transfers between devices: 782 us -> 333 us
  matrix products: 338 us -> 123 us
  local copies, waits for them, and re-layouts: 235 us -> 34 us
  Pallas kernels: 0 us -> 101 us
  blocking collectives: 56.6 us -> 0 us
  starting transfers between devices: 2.34 us -> 53.2 us
    psum x3 -> x0, waiting for transfers between devices: 343 us -> none  [grid_total(): summed = lax.psum(partial_value, 'row')]
    ppermute x0 -> x65, waiting for transfers between devices: none -> 333 us  [the longest x26 119 us: to_row(): return lax.ppermute(v, 'row', [(i, i ^ k) for i in range(rows)])]
    another operation x97 -> x1, other arithmetic: 322 us -> 0.08 us  [body(): half_of = jnp.stack([c, 1 - c]).astype(jnp.int32)]
    reduce_scatter x13 -> x0, waiting for transfers between devices: 310 us -> none  [the longest x1 57 us: body(): lax.psum_scatter(down_grad.astype(jnp.bfloat16), 'dp', scatter_dimension=...]
    dot_general x376 -> x41, matrix products: 318 us -> 123 us  [mm(): return lax.dot_general(left, right, dims, preferred_element_type=F32)]
    pallas_call x0 -> x6, Pallas kernels: none -> 101 us  [the longest x1 50.2 us: delta_forward(): pl.pallas_call(functools.partial(fwd_kernel, heads, chunks, *dots), out_s...]
    convert_element_type x86 -> x8, other arithmetic: 103 us -> 5.24 us  [the longest x1 2.61 us: body(): input_grad = row_gather((d_middle + d_norm).astype(BF16))]
    all_gather x10 -> x0, waiting for transfers between devices: 91.6 us -> none  [the longest x4 55 us: grid_total(): return lax.all_gather(summed, 'col', axis=1, tiled=True)]
  transfers between devices with their start and end apart: 30 -> 65, of which waited for: 23 -> 21; matrix products, arithmetic and copies ran while one was open for 31% -> 24% of each run, Pallas kernels for 0% -> 15%
where the time goes in v1:
time: 676 us; the launch traced here: 667 us
  waiting for transfers between devices  333 us (49%)
  matrix products  123 us (18%)
  Pallas kernels  101 us (15%)
  starting transfers between devices  53.2 us (8%)
  local copies, waits for them, and re-layouts  34 us (5%)
  other arithmetic  19.1 us (3%)
    dot_general x41, matrix products, mm(): return lax.dot_general(left, right, dims, preferred_element_type=F32)  123 us
    ppermute x26, waiting for transfers between devices, to_row(): return lax.ppermute(v, 'row', [(i, i ^ k) for i in range(rows)])  119 us
    ppermute x2, waiting for transfers between devices, all_sum(): v = v + lax.ppermute(v, 'dp', [(i, i ^ k) for i in range(groups)])  116 us
    ppermute x10, waiting for transfers between devices, group_sum(): got = lax.ppermute(send, 'dp', [(i, i ^ step) for i in range(groups)])  96.3 us
    pallas_call x1, Pallas kernels, delta_forward(): pl.pallas_call(functools.partial(fwd_kernel, heads, chunks, *dots), out_s...  50.2 us
    pallas_call x1, Pallas kernels, delta_backward(): pl.pallas_call(functools.partial(bwd_kernel, heads, chunks, *dots), out_s...  38.4 us
    ppermute x26, starting transfers between devices, to_row(): return lax.ppermute(v, 'row', [(i, i ^ k) for i in range(rows)])  32.5 us
  transfers between devices with their start and end apart: 65, of which 21 were waited for; matrix products, arithmetic and copies ran while one was open for 24% of the time, Pallas kernels for 15%

profile of v1, /device:TPU:0, one launch (start us, length us, event | category | flops | bytes accessed | tf_op | source)
XLA Modules:
  0.0 666.6 jit_solution(10943414857831066211)
XLA Ops:
  8.2 2.2 copy-done.1
  12.6 3.0 ordered_rows.2
  18.4 3.8 fusion.29
  22.3 5.8 fusion.21.z_ref
  28.1 50.2 %delta_forward.1 = (bf16[1024,256]{1,0:T(8,128)(2,1)S(1)}, f32[1024,256]{1,0:T(8,128)S(1)}, f32[16,128,128]{2,1,0:T(8,128)S(1)}, f32[16,128,128]{2,1,0:T(8,128)S...) custom-call(s32[8]{0:T(128)S(1)} %fusion.119.place, ...), custom_call_target="tpu_custom_call" | custom-call | flops 60000002048 | bytes 16000000 | tf_op jit(solution)/shard_map/delta_forward/pallas_call | solution.py:181
  82.6 2.7 collective-permute-start.5
  86.8 3.8 fusion.63
  90.6 7.4 %collective-permute-done.5 = bf16[128,2048]{1,0:T(8,128)(2,1)S(1)} collective-permute-done((bf16[128,2048]{1,0:T(8,128)(2,1)S(1)}, bf16[128,2048]{1,0:T(8,128)(2,1)S(1)}, u32[]{:S(2)}, u32[]{:S(2)}) %collective-permute-start.5) | collective-permute-done | bytes 524320 | tf_op jit(solution)/shard_map/ppermute | solution.py:416
  98.0 12.4 %collective-permute-done.4 = bf16[128,2048]{1,0:T(8,128)(2,1)S(1)} collective-permute-done((bf16[128,2048]{1,0:T(8,128)(2,1)S(1)}, bf16[128,2048]{1,0:T(8,128)(2,1)S(1)}, u32[]{:S(2)}, u32[]{:S(2)}) %collective-permute-start.4) | collective-permute-done | bytes 524320 | tf_op jit(solution)/shard_map/ppermute | solution.py:416
  115.1 3.7 convolution_add_fusion
  118.7 8.6 %collective-permute-done.8 = bf16[128,2048]{1,0:T(8,128)(2,1)S(1)} collective-permute-done((bf16[128,2048]{1,0:T(8,128)(2,1)S(1)}, bf16[128,2048]{1,0:T(8,128)(2,1)S(1)}, u32[]{:S(2)}, u32[]{:S(2)}) %collective-permute-start.8) | collective-permute-done | bytes 524320 | tf_op jit(solution)/shard_map/ppermute | solution.py:416
  127.4 9.6 %collective-permute-done.7 = bf16[128,2048]{1,0:T(8,128)(2,1)S(1)} collective-permute-done((bf16[128,2048]{1,0:T(8,128)(2,1)S(1)}, bf16[128,2048]{1,0:T(8,128)(2,1)S(1)}, u32[]{:S(2)}, u32[]{:S(2)}) %collective-permute-start.7) | collective-permute-done | bytes 524320 | tf_op jit(solution)/shard_map/ppermute | solution.py:416
  137.1 4.4 fusion.125
  141.5 3.6 convolution_add_fusion.1
  147.0 4.7 multiply_convert_fusion.1
  151.7 3.2 fusion.57
  156.9 3.3 convolution_convert_fusion.3
  160.2 3.3 fusion.99
  163.4 3.6 add_convert_fusion.7
  167.0 3.6 fusion.53
  170.6 2.7 add_convert_fusion.6
  176.9 3.0 convolution_add_fusion.5
  179.9 3.0 fusion.91
  185.0 3.2 fusion.97
  188.2 3.2 convolution_convert_fusion.2
  191.5 8.7 %collective-permute-done.23 = bf16[128,2048]{1,0:T(8,128)(2,1)S(1)} collective-permute-done((bf16[128,2048]{1,0:T(8,128)(2,1)S(1)}, bf16[128,2048]{1,0:T(8,128)(2,1)S(1)}, u32[]{:S(2)}, u32[]{:S(2)}) %collective-permute-start.23) | collective-permute-done | bytes 524320 | tf_op jit(solution)/shard_map/ppermute | solution.py:416
  206.9 4.1 fusion.61
  211.1 5.9 collective-permute-done.27
  217.0 9.6 %collective-permute-done.26 = bf16[128,2048]{1,0:T(8,128)(2,1)S(1)} collective-permute-done((bf16[128,2048]{1,0:T(8,128)(2,1)S(1)}, bf16[128,2048]{1,0:T(8,128)(2,1)S(1)}, u32[]{:S(2)}, u32[]{:S(2)}) %collective-permute-start.26) | collective-permute-done | bytes 524320 | tf_op jit(solution)/shard_map/ppermute | solution.py:416
  230.2 38.4 %delta_backward.1 = (bf16[1024,896]{1,0:T(8,128)(2,1)}, f32[4,768]{1,0:T(4,128)S(1)}, f32[1,128]{1,0:T(1,128)S(1)}) custom-call(s32[8]{0:T(128)S(1)} %fusion.119.place, bf16[1024,256]{1,0:T(8,128)(2,1)S(1)} %pad_maximum_fusion.6.dh_ref, f32[1024,896]{1,0:T(8,128)} %fusion.21.z_ref, f32[4,768]{1,0:T(4,128)S(1)} %pad_maximum_fusion.7.taps_ref, ...), custom_call_target="tpu_custom_call" | custom-call | flops 49999998976 | bytes 16000000 | tf_op jit(solution)/shard_map/delta_backward/pallas_call | solution.py:318
  268.6 5.4 convolution_convert_fusion.1
  275.6 3.7 fusion.73
  280.7 2.7 collective-permute-start.50
  283.4 2.2 fusion.105
  285.6 3.0 copy.48
  290.4 3.5 fusion.142
  294.1 3.6 fusion.143
  297.7 3.5 add_convert_fusion.2
  301.2 4.4 add_convert_fusion.1
  306.1 3.6 add_convert_fusion
  320.2 2.5 fusion.69
  322.7 3.1 add_convert_fusion.4
  330.5 3.7 fusion.24
  334.2 3.6 copy.49
  337.8 2.3 fusion.101
  340.1 2.5 convolution_add_fusion.6
  346.0 18.1 %collective-permute-done.32 = bf16[128,2048]{1,0:T(8,128)(2,1)} collective-permute-done((bf16[128,2048]{1,0:T(8,128)(2,1)}, bf16[128,2048]{1,0:T(8,128)(2,1)}, u32[]{:S(2)}, u32[]{:S(2)}) %collective-permute-start.32) | collective-permute-done | bytes 524320 | tf_op jit(solution)/shard_map/ppermute | solution.py:416
  369.5 6.3 collective-permute-done.53
  377.4 2.2 collective-permute-done.42
  381.0 2.4 collective-permute-done.43
  383.4 21.2 %collective-permute-done.44 = f32[33,128]{1,0:T(8,128)S(1)} collective-permute-done((f32[33,128]{1,0:T(8,128)S(1)}, f32[33,128]{1,0:T(8,128)S(1)}, u32[]{:S(2)}, u32[]{:S(2)}) %collective-permute-start.44) | collective-permute-done | bytes 16928 | tf_op jit(solution)/shard_map/ppermute | solution.py:457
  407.5 2.6 fusion.38
  410.1 95.3 %collective-permute-done.45 = f32[33,128]{1,0:T(8,128)S(1)} collective-permute-done((f32[33,128]{1,0:T(8,128)S(1)}, f32[33,128]{1,0:T(8,128)S(1)}, u32[]{:S(2)}, u32[]{:S(2)}) %collective-permute-start.45) | collective-permute-done | bytes 16928 | tf_op jit(solution)/shard_map/ppermute | solution.py:457
  505.4 3.4 collective-permute-start.54
  512.0 5.3 collective-permute-done.54
  522.7 18.2 %collective-permute-done.16.refs_2_ = bf16[128,2048]{1,0:T(8,128)(2,1)S(1)} collective-permute-done((bf16[128,2048]{1,0:T(8,128)(2,1)S(1)}, bf16[128,2048]{1,0:T(8,128)(2,1)S(1)}, u32[]{:S(2)}, u32[]{:S(2)}) %collective-permute-start.16) | collective-permute-done | bytes 524320 | tf_op jit(solution)/shard_map/ppermute | solution.py:416
  543.8 2.9 collective-permute-start.64
  547.5 16.1 %collective-permute-done.35.refs_2_ = bf16[128,2048]{1,0:T(8,128)(2,1)S(1)} collective-permute-done((bf16[128,2048]{1,0:T(8,128)(2,1)S(1)}, bf16[128,2048]{1,0:T(8,128)(2,1)S(1)}, u32[]{:S(2)}, u32[]{:S(2)}) %collective-permute-start.35) | collective-permute-done | bytes 524320 | tf_op jit(solution)/shard_map/ppermute | solution.py:416
  564.2 27.8 %collective-permute-done.58 = bf16[1,256,1408]{2,1,0:T(8,128)(2,1)S(1)} collective-permute-done((bf16[1,256,1408]{2,1,0:T(8,128)(2,1)S(1)}, bf16[1,256,1408]{2,1,0:T(8,128)(2,1)S(1)}, u32[]{:S(2)}, u32[]{:S(2)}) %collective-permute-start.58) | collective-permute-done | bytes 720928 | tf_op jit(solution)/shard_map/ppermute | solution.py:441
  592.0 15.4 %collective-permute-done.64 = bf16[1,352,1024]{2,1,0:T(8,128)(2,1)S(1)} collective-permute-done((bf16[1,352,1024]{2,1,0:T(8,128)(2,1)S(1)}, bf16[1,352,1024]{2,1,0:T(8,128)(2,1)S(1)}, u32[]{:S(2)}, u32[]{:S(2)}) %collective-permute-start.64) | collective-permute-done | bytes 720928 | tf_op jit(solution)/shard_map/ppermute | solution.py:441
  610.0 22.7 %collective-permute-done.61 = bf16[1,256,1408]{2,1,0:T(8,128)(2,1)S(1)} collective-permute-done((bf16[1,256,1408]{2,1,0:T(8,128)(2,1)S(1)}, bf16[1,256,1408]{2,1,0:T(8,128)(2,1)S(1)}, u32[]{:S(2)}, u32[]{:S(2)}) %collective-permute-start.61) | collective-permute-done | bytes 720928 | tf_op jit(solution)/shard_map/ppermute | solution.py:441
  635.0 4.2 place_rows.2
  639.2 4.2 place_rows.3
  643.3 18.8 %collective-permute-done.48 = bf16[1,256,1792]{1,2,0:T(8,128)(2,1)S(1)} collective-permute-done((bf16[1,256,1792]{1,2,0:T(8,128)(2,1)S(1)}, bf16[1,256,1792]{1,2,0:T(8,128)(2,1)S(1)}, u32[]{:S(2)}, u32[]{:S(2)}) %collective-permute-start.48) | collective-permute-done | bytes 917536 | tf_op jit(solution)/shard_map/ppermute | solution.py:441
  (337 shorter events, 99.3 us)
Async XLA Ops:
  5.6 16.6 %collective-permute-start = (bf16[1024,896]{1,0:T(8,128)(2,1)S(1)}, bf16[1024,896]{1,0:T(8,128)(2,1)}, u32[]{:S(2)}, u32[]{:S(2)}) collective-permute-start(bf16[1024,896]{1,0:T(8,128)(2,1)S(1)} %fusion.12), channel_id=1, source_target_pairs={{0,1},{1,0},{2,3},{3,2},{4,5},{5,4},{6,7},{7,6},{8,9},{9,8},{10,11... | collective-permute-start | bytes 5505032 | tf_op jit(solution)/shard_map/ppermute | solution.py:413
  6.2 73.9 %collective-permute-start.2 = (bf16[512,1024]{1,0:T(8,128)(2,1)}, bf16[512,1024]{1,0:T(8,128)(2,1)}, u32[]{:S(2)}, u32[]{:S(2)}) collective-permute-start(bf16[512,1024]{1,0:T(8,128)(2,1)} %param.28), channel_id=1, source_target_pairs={{0,1},{1,0},{2,3},{3,2},{4,5},{5,4},{6,7},{7,6},{8,9},{9,8},{10,11... | collective-permute-start | bytes 3145736 | tf_op jit(solution)/shard_map/ppermute | solution.py:413
  6.2 108.0 %collective-permute-start.11 = (bf16[1408,1024]{1,0:T(8,128)(2,1)}, bf16[1408,1024]{1,0:T(8,128)(2,1)}, u32[]{:S(2)}, u32[]{:S(2)}) collective-permute-start(bf16[1408,1024]{1,0:T(8,128)(2,1)} %param.32), channel_id=1, source_target_pairs={{0,1},{1,0},{2,3},{3,2},{4,5},{5,4},{6,7},{7,6},{8,9},{9,8},{10,11... | collective-permute-start | bytes 8650760 | tf_op jit(solution)/shard_map/ppermute | solution.py:413
  6.7 130.5 %collective-permute-start.10 = (bf16[1024,1408]{1,0:T(8,128)(2,1)}, bf16[1024,1408]{1,0:T(8,128)(2,1)}, u32[]{:S(2)}, u32[]{:S(2)}) collective-permute-start(bf16[1024,1408]{1,0:T(8,128)(2,1)} %param.31), channel_id=1, source_target_pairs={{0,1},{1,0},{2,3},{3,2},{4,5},{5,4},{6,7},{7,6},{8,9},{9,8},{10,11... | collective-permute-start | bytes 8650760 | tf_op jit(solution)/shard_map/ppermute | solution.py:413
  78.3 3.1 collective-permute-start.1
  82.6 15.4 %collective-permute-start.5 = (bf16[128,2048]{1,0:T(8,128)(2,1)S(1)}, bf16[128,2048]{1,0:T(8,128)(2,1)S(1)}, u32[]{:S(2)}, u32[]{:S(2)}) collective-permute-start(bf16[128,2048]{1,0:T(8,128)(2,1)S(1)} %get-tuple-element.101), channel_id=1, source_target_pairs={{0,2},{2,0},{4,6},{6,4},{1,3},{3,1},{5,7},{7,5},{8,10},{10,8},{12,... | collective-permute-start | bytes 1572872 | tf_op jit(solution)/shard_map/ppermute | solution.py:416
  85.2 25.2 %collective-permute-start.4 = (bf16[128,2048]{1,0:T(8,128)(2,1)S(1)}, bf16[128,2048]{1,0:T(8,128)(2,1)S(1)}, u32[]{:S(2)}, u32[]{:S(2)}) collective-permute-start(bf16[128,2048]{1,0:T(8,128)(2,1)S(1)} %get-tuple-element.102), channel_id=1, source_target_pairs={{0,4},{2,6},{4,0},{6,2},{1,5},{3,7},{5,1},{7,3},{8,12},{10,14},{12... | collective-permute-start | bytes 1572872 | tf_op jit(solution)/shard_map/ppermute | solution.py:416
  86.7 23.7 %collective-permute-start.3 = (bf16[128,2048]{1,0:T(8,128)(2,1)S(1)}, bf16[128,2048]{1,0:T(8,128)(2,1)S(1)}, u32[]{:S(2)}, u32[]{:S(2)}) collective-permute-start(bf16[128,2048]{1,0:T(8,128)(2,1)S(1)} %get-tuple-element.100), channel_id=1, source_target_pairs={{0,6},{2,4},{4,2},{6,0},{1,7},{3,5},{5,3},{7,1},{8,14},{10,12},{12... | collective-permute-start | bytes 1572872 | tf_op jit(solution)/shard_map/ppermute | solution.py:416
  98.0 47.2 %collective-permute-start.9 = (bf16[1024,1408]{1,0:T(8,128)(2,1)S(1)}, bf16[1024,1408]{1,0:T(8,128)(2,1)S(1)}, u32[]{:S(2)}, u32[]{:S(2)}) collective-permute-start(bf16[1024,1408]{1,0:T(8,128)(2,1)S(1)} %copy-done.34), channel_id=1, source_target_pairs={{0,1},{1,0},{2,3},{3,2},{4,5},{5,4},{6,7},{7,6},{8,9},{9,8},{10,11... | collective-permute-start | bytes 8650760 | tf_op jit(solution)/shard_map/ppermute | solution.py:413
  111.5 15.9 %collective-permute-start.8 = (bf16[128,2048]{1,0:T(8,128)(2,1)S(1)}, bf16[128,2048]{1,0:T(8,128)(2,1)S(1)}, u32[]{:S(2)}, u32[]{:S(2)}) collective-permute-start(bf16[128,2048]{1,0:T(8,128)(2,1)S(1)} %multiply_convert_fusion.3), channel_id=1, source_target_pairs={{0,6},{2,4},{4,2},{6,0},{1,7},{3,5},{5,3},{7,1},{8,14},{10,12},{12... | collective-permute-start | bytes 1572872 | tf_op jit(solution)/shard_map/ppermute | solution.py:416
  113.1 23.9 %collective-permute-start.7 = (bf16[128,2048]{1,0:T(8,128)(2,1)S(1)}, bf16[128,2048]{1,0:T(8,128)(2,1)S(1)}, u32[]{:S(2)}, u32[]{:S(2)}) collective-permute-start(bf16[128,2048]{1,0:T(8,128)(2,1)S(1)} %multiply_convert_fusion.3), channel_id=1, source_target_pairs={{0,4},{2,6},{4,0},{6,2},{1,5},{3,7},{5,1},{7,3},{8,12},{10,14},{12... | collective-permute-start | bytes 1572872 | tf_op jit(solution)/shard_map/ppermute | solution.py:416
  114.3 22.7 %collective-permute-start.6 = (bf16[128,2048]{1,0:T(8,128)(2,1)S(1)}, bf16[128,2048]{1,0:T(8,128)(2,1)S(1)}, u32[]{:S(2)}, u32[]{:S(2)}) collective-permute-start(bf16[128,2048]{1,0:T(8,128)(2,1)S(1)} %multiply_convert_fusion.3), channel_id=1, source_target_pairs={{0,2},{2,0},{4,6},{6,4},{1,3},{3,1},{5,7},{7,5},{8,10},{10,8},{12,... | collective-permute-start | bytes 1572872 | tf_op jit(solution)/shard_map/ppermute | solution.py:416
  127.4 192.8 %collective-permute-start.30 = (bf16[1024,896]{1,0:T(8,128)(2,1)}, bf16[1024,896]{1,0:T(8,128)(2,1)}, u32[]{:S(2)}, u32[]{:S(2)}) collective-permute-start(bf16[1024,896]{1,0:T(8,128)(2,1)} %fusion.11), channel_id=1, source_target_pairs={{0,1},{1,0},{2,3},{3,2},{4,5},{5,4},{6,7},{7,6},{8,9},{9,8},{10,11... | collective-permute-start | bytes 5505032 | tf_op jit(solution)/shard_map/ppermute | solution.py:413
  163.4 126.4 %collective-permute-start.56 = (bf16[512,1408]{1,0:T(8,128)(2,1)}, bf16[512,1408]{1,0:T(8,128)(2,1)}, u32[]{:S(2)}, u32[]{:S(2)}) collective-permute-start(bf16[512,1408]{1,0:T(8,128)(2,1)} %get-tuple-element.76), channel_id=1, source_target_pairs={{0,1},{1,0},{2,3},{3,2},{4,5},{5,4},{6,7},{7,6},{8,9},{9,8},{10,11... | collective-permute-start | bytes 4325384 | tf_op jit(solution)/shard_map/ppermute | solution.py:413
  173.4 18.1 %collective-permute-start.24 = (bf16[128,2048]{1,0:T(8,128)(2,1)S(1)}, bf16[128,2048]{1,0:T(8,128)(2,1)S(1)}, u32[]{:S(2)}, u32[]{:S(2)}) collective-permute-start(bf16[128,2048]{1,0:T(8,128)(2,1)S(1)} %get-tuple-element.95), channel_id=1, source_target_pairs={{0,2},{2,0},{4,6},{6,4},{1,3},{3,1},{5,7},{7,5},{8,10},{10,8},{12,... | collective-permute-start | bytes 1572872 | tf_op jit(solution)/shard_map/ppermute | solution.py:416
  174.9 25.3 %collective-permute-start.23 = (bf16[128,2048]{1,0:T(8,128)(2,1)S(1)}, bf16[128,2048]{1,0:T(8,128)(2,1)S(1)}, u32[]{:S(2)}, u32[]{:S(2)}) collective-permute-start(bf16[128,2048]{1,0:T(8,128)(2,1)S(1)} %get-tuple-element.96), channel_id=1, source_target_pairs={{0,4},{2,6},{4,0},{6,2},{1,5},{3,7},{5,1},{7,3},{8,12},{10,14},{12... | collective-permute-start | bytes 1572872 | tf_op jit(solution)/shard_map/ppermute | solution.py:416
  175.4 24.7 %collective-permute-start.22 = (bf16[128,2048]{1,0:T(8,128)(2,1)S(1)}, bf16[128,2048]{1,0:T(8,128)(2,1)S(1)}, u32[]{:S(2)}, u32[]{:S(2)}) collective-permute-start(bf16[128,2048]{1,0:T(8,128)(2,1)S(1)} %get-tuple-element.94), channel_id=1, source_target_pairs={{0,6},{2,4},{4,2},{6,0},{1,7},{3,5},{5,3},{7,1},{8,14},{10,12},{12... | collective-permute-start | bytes 1572872 | tf_op jit(solution)/shard_map/ppermute | solution.py:416
  201.1 15.9 %collective-permute-start.27 = (bf16[128,2048]{1,0:T(8,128)(2,1)S(1)}, bf16[128,2048]{1,0:T(8,128)(2,1)S(1)}, u32[]{:S(2)}, u32[]{:S(2)}) collective-permute-start(bf16[128,2048]{1,0:T(8,128)(2,1)S(1)} %fusion.129), channel_id=1, source_target_pairs={{0,6},{2,4},{4,2},{6,0},{1,7},{3,5},{5,3},{7,1},{8,14},{10,12},{12... | collective-permute-start | bytes 1572872 | tf_op jit(solution)/shard_map/ppermute | solution.py:416
  202.6 24.0 %collective-permute-start.26 = (bf16[128,2048]{1,0:T(8,128)(2,1)S(1)}, bf16[128,2048]{1,0:T(8,128)(2,1)S(1)}, u32[]{:S(2)}, u32[]{:S(2)}) collective-permute-start(bf16[128,2048]{1,0:T(8,128)(2,1)S(1)} %fusion.129), channel_id=1, source_target_pairs={{0,4},{2,6},{4,0},{6,2},{1,5},{3,7},{5,1},{7,3},{8,12},{10,14},{12... | collective-permute-start | bytes 1572872 | tf_op jit(solution)/shard_map/ppermute | solution.py:416
  203.2 23.4 %collective-permute-start.25 = (bf16[128,2048]{1,0:T(8,128)(2,1)S(1)}, bf16[128,2048]{1,0:T(8,128)(2,1)S(1)}, u32[]{:S(2)}, u32[]{:S(2)}) collective-permute-start(bf16[128,2048]{1,0:T(8,128)(2,1)S(1)} %fusion.129), channel_id=1, source_target_pairs={{0,2},{2,0},{4,6},{6,4},{1,3},{3,1},{5,7},{7,5},{8,10},{10,8},{12,... | collective-permute-start | bytes 1572872 | tf_op jit(solution)/shard_map/ppermute | solution.py:416
  217.0 77.0 %collective-permute-start.59 = (bf16[512,1408]{1,0:T(8,128)(2,1)}, bf16[512,1408]{1,0:T(8,128)(2,1)}, u32[]{:S(2)}, u32[]{:S(2)}) collective-permute-start(bf16[512,1408]{1,0:T(8,128)(2,1)} %get-tuple-element.78), channel_id=1, source_target_pairs={{0,1},{1,0},{2,3},{3,2},{4,5},{5,4},{6,7},{7,6},{8,9},{9,8},{10,11... | collective-permute-start | bytes 4325384 | tf_op jit(solution)/shard_map/ppermute | solution.py:413
  226.6 62.7 %collective-permute-start.55 = (bf16[512,1024]{1,0:T(8,128)(2,1)}, bf16[512,1024]{1,0:T(8,128)(2,1)}, u32[]{:S(2)}, u32[]{:S(2)}) collective-permute-start(bf16[512,1024]{1,0:T(8,128)(2,1)} %slice.220), channel_id=1, source_target_pairs={{0,1},{1,0},{2,3},{3,2},{4,5},{5,4},{6,7},{7,6},{8,9},{9,8},{10,11... | collective-permute-start | bytes 3145736 | tf_op jit(solution)/shard_map/ppermute | solution.py:413
  228.1 2.0 collective-permute-start.28
  274.0 6.7 %collective-permute-start.49 = (f32[4,768]{1,0:T(4,128)S(1)}, f32[4,768]{1,0:T(4,128)S(1)}, u32[]{:S(2)}, u32[]{:S(2)}) collective-permute-start(f32[4,768]{1,0:T(4,128)S(1)} %get-tuple-element.37), channel_id=1, source_target_pairs={{0,8},{8,0},{16,24},{24,16},{1,9},{9,1},{17,25},{25,17},{2,10},{10... | collective-permute-start | bytes 36872 | tf_op jit(solution)/shard_map/ppermute | solution.py:575
  280.7 7.8 %collective-permute-start.50 = (f32[4,768]{1,0:T(4,128)S(1)}, f32[4,768]{1,0:T(4,128)S(1)}, u32[]{:S(2)}, u32[]{:S(2)}) collective-permute-start(f32[4,768]{1,0:T(4,128)S(1)} %add.381), channel_id=1, source_target_pairs={{0,16},{8,24},{16,0},{24,8},{1,17},{9,25},{17,1},{25,9},{2,18},{10... | collective-permute-start | bytes 36872 | tf_op jit(solution)/shard_map/ppermute | solution.py:575
  288.6 25.0 %collective-permute-start.51 = (bf16[512,256]{1,0:T(8,128)(2,1)}, bf16[512,256]{1,0:T(8,128)(2,1)S(1)}, u32[]{:S(2)}, u32[]{:S(2)}) collective-permute-start(bf16[512,256]{1,0:T(8,128)(2,1)} %copy-done.47), channel_id=1, source_target_pairs={{0,1},{1,0},{2,3},{3,2},{4,5},{5,4},{6,7},{7,6},{8,9},{9,8},{10,11... | collective-permute-start | bytes 786440 | tf_op jit(solution)/shard_map/ppermute | solution.py:413
  289.3 16.3 %collective-permute-start.62 = (bf16[512,1408]{1,0:T(8,128)(2,1)}, bf16[512,1408]{1,0:T(8,128)(2,1)S(1)}, u32[]{:S(2)}, u32[]{:S(2)}) collective-permute-start(bf16[512,1408]{1,0:T(8,128)(2,1)} %copy-done.55), channel_id=1, source_target_pairs={{0,1},{1,0},{2,3},{3,2},{4,5},{5,4},{6,7},{7,6},{8,9},{9,8},{10,11... | collective-permute-start | bytes 4325384 | tf_op jit(solution)/shard_map/ppermute | solution.py:413
  289.8 115.2 %collective-permute-start.14 = (bf16[128,2048]{1,0:T(8,128)(2,1)}, bf16[128,2048]{1,0:T(8,128)(2,1)}, u32[]{:S(2)}, u32[]{:S(2)}) collective-permute-start(bf16[128,2048]{1,0:T(8,128)(2,1)} %get-tuple-element.98), channel_id=1, source_target_pairs={{0,2},{2,0},{4,6},{6,4},{1,3},{3,1},{5,7},{7,5},{8,10},{10,8},{12,... | collective-permute-start | bytes 1572872 | tf_op jit(solution)/shard_map/ppermute | solution.py:416
  294.0 20.9 %collective-permute-start.52 = (bf16[512,1024]{1,0:T(8,128)(2,1)S(1)}, bf16[512,1024]{1,0:T(8,128)(2,1)S(1)}, u32[]{:S(2)}, u32[]{:S(2)}) collective-permute-start(bf16[512,1024]{1,0:T(8,128)(2,1)S(1)} %copy-done.46), channel_id=1, source_target_pairs={{0,1},{1,0},{2,3},{3,2},{4,5},{5,4},{6,7},{7,6},{8,9},{9,8},{10,11... | collective-permute-start | bytes 3145736 | tf_op jit(solution)/shard_map/ppermute | solution.py:413
  305.7 12.5 %collective-permute-start.29 = (bf16[512,896]{1,0:T(8,128)(2,1)S(1)}, bf16[512,896]{1,0:T(8,128)(2,1)S(1)}, u32[]{:S(2)}, u32[]{:S(2)}) collective-permute-start(bf16[512,896]{1,0:T(8,128)(2,1)S(1)} %copy-done.52), channel_id=1, source_target_pairs={{0,1},{1,0},{2,3},{3,2},{4,5},{5,4},{6,7},{7,6},{8,9},{9,8},{10,11... | collective-permute-start | bytes 2752520 | tf_op jit(solution)/shard_map/ppermute | solution.py:413
  313.5 93.2 %collective-permute-start.13 = (bf16[128,2048]{1,0:T(8,128)(2,1)}, bf16[128,2048]{1,0:T(8,128)(2,1)}, u32[]{:S(2)}, u32[]{:S(2)}) collective-permute-start(bf16[128,2048]{1,0:T(8,128)(2,1)} %get-tuple-element.99), channel_id=1, source_target_pairs={{0,4},{2,6},{4,0},{6,2},{1,5},{3,7},{5,1},{7,3},{8,12},{10,14},{12... | collective-permute-start | bytes 1572872 | tf_op jit(solution)/shard_map/ppermute | solution.py:416
  314.9 14.1 %collective-permute-start.46 = (bf16[512,896]{1,0:T(8,128)(2,1)S(1)}, bf16[512,896]{1,0:T(8,128)(2,1)S(1)}, u32[]{:S(2)}, u32[]{:S(2)}) collective-permute-start(bf16[512,896]{1,0:T(8,128)(2,1)S(1)} %copy-done.51), channel_id=1, source_target_pairs={{0,1},{1,0},{2,3},{3,2},{4,5},{5,4},{6,7},{7,6},{8,9},{9,8},{10,11... | collective-permute-start | bytes 2752520 | tf_op jit(solution)/shard_map/ppermute | solution.py:413
  327.0 17.4 %collective-permute-start.33 = (bf16[128,2048]{1,0:T(8,128)(2,1)}, bf16[128,2048]{1,0:T(8,128)(2,1)}, u32[]{:S(2)}, u32[]{:S(2)}) collective-permute-start(bf16[128,2048]{1,0:T(8,128)(2,1)} %get-tuple-element.92), channel_id=1, source_target_pairs={{0,2},{2,0},{4,6},{6,4},{1,3},{3,1},{5,7},{7,5},{8,10},{10,8},{12,... | collective-permute-start | bytes 1572872 | tf_op jit(solution)/shard_map/ppermute | solution.py:416
  327.6 36.4 %collective-permute-start.32 = (bf16[128,2048]{1,0:T(8,128)(2,1)}, bf16[128,2048]{1,0:T(8,128)(2,1)}, u32[]{:S(2)}, u32[]{:S(2)}) collective-permute-start(bf16[128,2048]{1,0:T(8,128)(2,1)} %get-tuple-element.93), channel_id=1, source_target_pairs={{0,4},{2,6},{4,0},{6,2},{1,5},{3,7},{5,1},{7,3},{8,12},{10,14},{12... | collective-permute-start | bytes 1572872 | tf_op jit(solution)/shard_map/ppermute | solution.py:416
  329.0 35.5 %collective-permute-start.31 = (bf16[128,2048]{1,0:T(8,128)(2,1)}, bf16[128,2048]{1,0:T(8,128)(2,1)}, u32[]{:S(2)}, u32[]{:S(2)}) collective-permute-start(bf16[128,2048]{1,0:T(8,128)(2,1)} %get-tuple-element.91), channel_id=1, source_target_pairs={{0,6},{2,4},{4,2},{6,0},{1,7},{3,5},{5,3},{7,1},{8,14},{10,12},{12... | collective-permute-start | bytes 1572872 | tf_op jit(solution)/shard_map/ppermute | solution.py:416
  344.5 62.7 %collective-permute-start.12 = (bf16[128,2048]{1,0:T(8,128)(2,1)S(1)}, bf16[128,2048]{1,0:T(8,128)(2,1)S(1)}, u32[]{:S(2)}, u32[]{:S(2)}) collective-permute-start(bf16[128,2048]{1,0:T(8,128)(2,1)S(1)} %copy-done.54), channel_id=1, source_target_pairs={{0,6},{2,4},{4,2},{6,0},{1,7},{3,5},{5,3},{7,1},{8,14},{10,12},{12... | collective-permute-start | bytes 1572872 | tf_op jit(solution)/shard_map/ppermute | solution.py:416
  364.0 11.8 %collective-permute-start.53 = (bf16[2,128,1024]{2,1,0:T(8,128)(2,1)S(1)}, bf16[2,128,1024]{2,1,0:T(8,128)(2,1)S(1)}, u32[]{:S(2)}, u32[]{:S(2)}) collective-permute-start(bf16[2,128,1024]{2,1,0:T(8,128)(2,1)S(1)} %copy-done.53), channel_id=1, source_target_pairs={{0,8},{8,0},{16,24},{24,16},{1,9},{9,1},{17,25},{25,17},{2,10},{10... | collective-permute-start | bytes 1572872 | tf_op jit(solution)/shard_map/ppermute | solution.py:441
  367.9 142.0 %collective-permute-start.63 = (bf16[2,352,1024]{2,1,0:T(8,128)(2,1)S(1)}, bf16[2,352,1024]{2,1,0:T(8,128)(2,1)S(1)}, u32[]{:S(2)}, u32[]{:S(2)}) collective-permute-start(bf16[2,352,1024]{2,1,0:T(8,128)(2,1)S(1)} %copy-done.41), channel_id=1, source_target_pairs={{0,8},{8,0},{16,24},{24,16},{1,9},{9,1},{17,25},{25,17},{2,10},{10... | collective-permute-start | bytes 4325384 | tf_op jit(solution)/shard_map/ppermute | solution.py:441
  375.8 3.8 collective-permute-start.42
  379.6 3.8 collective-permute-start.43
  383.4 21.2 %collective-permute-start.44 = (f32[33,128]{1,0:T(8,128)S(1)}, f32[33,128]{1,0:T(8,128)S(1)}, u32[]{:S(2)}, u32[]{:S(2)}) collective-permute-start(f32[33,128]{1,0:T(8,128)S(1)} %add.369), channel_id=1, source_target_pairs={{0,8},{8,0},{16,24},{24,16},{1,9},{9,1},{17,25},{25,17},{2,10},{10... | collective-permute-start | bytes 50696 | tf_op jit(solution)/shard_map/ppermute | solution.py:457
  404.6 114.9 %collective-permute-start.57 = (bf16[2,256,1408]{2,1,0:T(8,128)(2,1)S(1)}, bf16[2,256,1408]{2,1,0:T(8,128)(2,1)S(1)}, u32[]{:S(2)}, u32[]{:S(2)}) collective-permute-start(bf16[2,256,1408]{2,1,0:T(8,128)(2,1)S(1)} %copy-done.40), channel_id=1, source_target_pairs={{0,8},{8,0},{16,24},{24,16},{1,9},{9,1},{17,25},{25,17},{2,10},{10... | collective-permute-start | bytes 4325384 | tf_op jit(solution)/shard_map/ppermute | solution.py:441
  405.0 116.3 %collective-permute-start.60 = (bf16[2,256,1408]{2,1,0:T(8,128)(2,1)S(1)}, bf16[2,256,1408]{2,1,0:T(8,128)(2,1)S(1)}, u32[]{:S(2)}, u32[]{:S(2)}) collective-permute-start(bf16[2,256,1408]{2,1,0:T(8,128)(2,1)S(1)} %copy-done.39), channel_id=1, source_target_pairs={{0,8},{8,0},{16,24},{24,16},{1,9},{9,1},{17,25},{25,17},{2,10},{10... | collective-permute-start | bytes 4325384 | tf_op jit(solution)/shard_map/ppermute | solution.py:441
  406.7 137.1 %collective-permute-start.47 = (bf16[2,256,1792]{1,2,0:T(8,128)(2,1)S(1)}, bf16[2,256,1792]{1,2,0:T(8,128)(2,1)S(1)}, u32[]{:S(2)}, u32[]{:S(2)}) collective-permute-start(bf16[2,256,1792]{1,2,0:T(8,128)(2,1)S(1)} %fusion.14), channel_id=1, source_target_pairs={{0,8},{8,0},{16,24},{24,16},{1,9},{9,1},{17,25},{25,17},{2,10},{10... | collective-permute-start | bytes 5505032 | tf_op jit(solution)/shard_map/ppermute | solution.py:441
  407.1 98.2 %collective-permute-start.45 = (f32[33,128]{1,0:T(8,128)S(1)}, f32[33,128]{1,0:T(8,128)S(1)}, u32[]{:S(2)}, u32[]{:S(2)}) collective-permute-start(f32[33,128]{1,0:T(8,128)S(1)} %add.370), channel_id=1, source_target_pairs={{0,16},{8,24},{16,0},{24,8},{1,17},{9,25},{17,1},{25,9},{2,18},{10... | collective-permute-start | bytes 50696 | tf_op jit(solution)/shard_map/ppermute | solution.py:457
  505.4 11.9 %collective-permute-start.54 = (bf16[1,128,1024]{2,1,0:T(8,128)(2,1)S(1)}, bf16[1,128,1024]{2,1,0:T(8,128)(2,1)S(1)}, u32[]{:S(2)}, u32[]{:S(2)}) collective-permute-start(bf16[1,128,1024]{2,1,0:T(8,128)(2,1)S(1)} %constant_dynamic-slice_fusion.3), channel_id=1, source_target_pairs={{0,16},{8,24},{16,0},{24,8},{1,17},{9,25},{17,1},{25,9},{2,18},{10... | collective-permute-start | bytes 786440 | tf_op jit(solution)/shard_map/ppermute | solution.py:441
  509.9 12.1 %collective-permute-start.15 = (bf16[128,2048]{1,0:T(8,128)(2,1)S(1)}, bf16[128,2048]{1,0:T(8,128)(2,1)S(1)}, u32[]{:S(2)}, u32[]{:S(2)}) collective-permute-start(bf16[128,2048]{1,0:T(8,128)(2,1)S(1)} %get-tuple-element.104.refs_0_), channel_id=1, source_target_pairs={{0,2},{2,0},{4,6},{6,4},{1,3},{3,1},{5,7},{7,5},{8,10},{10,8},{12,... | collective-permute-start | bytes 1572872 | tf_op jit(solution)/shard_map/ppermute | solution.py:416
  517.3 23.7 %collective-permute-start.16 = (bf16[128,2048]{1,0:T(8,128)(2,1)S(1)}, bf16[128,2048]{1,0:T(8,128)(2,1)S(1)}, u32[]{:S(2)}, u32[]{:S(2)}) collective-permute-start(bf16[128,2048]{1,0:T(8,128)(2,1)S(1)} %get-tuple-element.104.refs_0_), channel_id=1, source_target_pairs={{0,4},{2,6},{4,0},{6,2},{1,5},{3,7},{5,1},{7,3},{8,12},{10,14},{12... | collective-permute-start | bytes 1572872 | tf_op jit(solution)/shard_map/ppermute | solution.py:416
  519.5 22.8 %collective-permute-start.17 = (bf16[128,2048]{1,0:T(8,128)(2,1)S(1)}, bf16[128,2048]{1,0:T(8,128)(2,1)S(1)}, u32[]{:S(2)}, u32[]{:S(2)}) collective-permute-start(bf16[128,2048]{1,0:T(8,128)(2,1)S(1)} %get-tuple-element.104.refs_0_), channel_id=1, source_target_pairs={{0,6},{2,4},{4,2},{6,0},{1,7},{3,5},{5,3},{7,1},{8,14},{10,12},{12... | collective-permute-start | bytes 1572872 | tf_op jit(solution)/shard_map/ppermute | solution.py:416
  521.4 22.5 %collective-permute-start.18 = (bf16[128,2048]{1,0:T(8,128)(2,1)S(1)}, bf16[128,2048]{1,0:T(8,128)(2,1)S(1)}, u32[]{:S(2)}, u32[]{:S(2)}) collective-permute-start(bf16[128,2048]{1,0:T(8,128)(2,1)S(1)} %get-tuple-element.104.refs_0_), channel_id=1, source_target_pairs={{0,1},{1,0},{2,3},{3,2},{4,5},{5,4},{6,7},{7,6},{8,9},{9,8},{10,11... | collective-permute-start | bytes 1572872 | tf_op jit(solution)/shard_map/ppermute | solution.py:413
  522.0 25.4 %collective-permute-start.34 = (bf16[128,2048]{1,0:T(8,128)(2,1)S(1)}, bf16[128,2048]{1,0:T(8,128)(2,1)S(1)}, u32[]{:S(2)}, u32[]{:S(2)}) collective-permute-start(bf16[128,2048]{1,0:T(8,128)(2,1)S(1)} %get-tuple-element.103.refs_0_), channel_id=1, source_target_pairs={{0,2},{2,0},{4,6},{6,4},{1,3},{3,1},{5,7},{7,5},{8,10},{10,8},{12,... | collective-permute-start | bytes 1572872 | tf_op jit(solution)/shard_map/ppermute | solution.py:416
  540.9 22.7 %collective-permute-start.35 = (bf16[128,2048]{1,0:T(8,128)(2,1)S(1)}, bf16[128,2048]{1,0:T(8,128)(2,1)S(1)}, u32[]{:S(2)}, u32[]{:S(2)}) collective-permute-start(bf16[128,2048]{1,0:T(8,128)(2,1)S(1)} %get-tuple-element.103.refs_0_), channel_id=1, source_target_pairs={{0,4},{2,6},{4,0},{6,2},{1,5},{3,7},{5,1},{7,3},{8,12},{10,14},{12... | collective-permute-start | bytes 1572872 | tf_op jit(solution)/shard_map/ppermute | solution.py:416
  542.3 21.4 %collective-permute-start.36 = (bf16[128,2048]{1,0:T(8,128)(2,1)S(1)}, bf16[128,2048]{1,0:T(8,128)(2,1)S(1)}, u32[]{:S(2)}, u32[]{:S(2)}) collective-permute-start(bf16[128,2048]{1,0:T(8,128)(2,1)S(1)} %get-tuple-element.103.refs_0_), channel_id=1, source_target_pairs={{0,6},{2,4},{4,2},{6,0},{1,7},{3,5},{5,3},{7,1},{8,14},{10,12},{12... | collective-permute-start | bytes 1572872 | tf_op jit(solution)/shard_map/ppermute | solution.py:416
  543.8 48.2 %collective-permute-start.58 = (bf16[1,256,1408]{2,1,0:T(8,128)(2,1)S(1)}, bf16[1,256,1408]{2,1,0:T(8,128)(2,1)S(1)}, u32[]{:S(2)}, u32[]{:S(2)}) collective-permute-start(bf16[1,256,1408]{2,1,0:T(8,128)(2,1)S(1)} %constant_dynamic-slice_fusion.2), channel_id=1, source_target_pairs={{0,16},{8,24},{16,0},{24,8},{1,17},{9,25},{17,1},{25,9},{2,18},{10... | collective-permute-start | bytes 2162696 | tf_op jit(solution)/shard_map/ppermute | solution.py:441
  543.8 63.6 %collective-permute-start.64 = (bf16[1,352,1024]{2,1,0:T(8,128)(2,1)S(1)}, bf16[1,352,1024]{2,1,0:T(8,128)(2,1)S(1)}, u32[]{:S(2)}, u32[]{:S(2)}) collective-permute-start(bf16[1,352,1024]{2,1,0:T(8,128)(2,1)S(1)} %constant_dynamic-slice_fusion), channel_id=1, source_target_pairs={{0,16},{8,24},{16,0},{24,8},{1,17},{9,25},{17,1},{25,9},{2,18},{10... | collective-permute-start | bytes 2162696 | tf_op jit(solution)/shard_map/ppermute | solution.py:441
  547.4 85.3 %collective-permute-start.61 = (bf16[1,256,1408]{2,1,0:T(8,128)(2,1)S(1)}, bf16[1,256,1408]{2,1,0:T(8,128)(2,1)S(1)}, u32[]{:S(2)}, u32[]{:S(2)}) collective-permute-start(bf16[1,256,1408]{2,1,0:T(8,128)(2,1)S(1)} %constant_dynamic-slice_fusion.1), channel_id=1, source_target_pairs={{0,16},{8,24},{16,0},{24,8},{1,17},{9,25},{17,1},{25,9},{2,18},{10... | collective-permute-start | bytes 2162696 | tf_op jit(solution)/shard_map/ppermute | solution.py:441
  563.7 69.0 %collective-permute-start.19 = (bf16[128,2048]{1,0:T(8,128)(2,1)S(1)}, bf16[128,2048]{1,0:T(8,128)(2,1)S(1)}, u32[]{:S(2)}, u32[]{:S(2)}) collective-permute-start(bf16[128,2048]{1,0:T(8,128)(2,1)S(1)} %collective-permute-done.15.refs_1_), channel_id=1, source_target_pairs={{0,1},{1,0},{2,3},{3,2},{4,5},{5,4},{6,7},{7,6},{8,9},{9,8},{10,11... | collective-permute-start | bytes 1572872 | tf_op jit(solution)/shard_map/ppermute | solution.py:413
  563.7 69.5 %collective-permute-start.20 = (bf16[128,2048]{1,0:T(8,128)(2,1)S(1)}, bf16[128,2048]{1,0:T(8,128)(2,1)S(1)}, u32[]{:S(2)}, u32[]{:S(2)}) collective-permute-start(bf16[128,2048]{1,0:T(8,128)(2,1)S(1)} %collective-permute-done.16.refs_2_), channel_id=1, source_target_pairs={{0,1},{1,0},{2,3},{3,2},{4,5},{5,4},{6,7},{7,6},{8,9},{9,8},{10,11... | collective-permute-start | bytes 1572872 | tf_op jit(solution)/shard_map/ppermute | solution.py:413
  592.0 41.3 %collective-permute-start.21 = (bf16[128,2048]{1,0:T(8,128)(2,1)S(1)}, bf16[128,2048]{1,0:T(8,128)(2,1)S(1)}, u32[]{:S(2)}, u32[]{:S(2)}) collective-permute-start(bf16[128,2048]{1,0:T(8,128)(2,1)S(1)} %collective-permute-done.17.refs_3_), channel_id=1, source_target_pairs={{0,1},{1,0},{2,3},{3,2},{4,5},{5,4},{6,7},{7,6},{8,9},{9,8},{10,11... | collective-permute-start | bytes 1572872 | tf_op jit(solution)/shard_map/ppermute | solution.py:413
  607.4 54.7 %collective-permute-start.48 = (bf16[1,256,1792]{1,2,0:T(8,128)(2,1)S(1)}, bf16[1,256,1792]{1,2,0:T(8,128)(2,1)S(1)}, u32[]{:S(2)}, u32[]{:S(2)}) collective-permute-start(bf16[1,256,1792]{1,2,0:T(8,128)(2,1)S(1)} %constant_dynamic-slice_fusion.7), channel_id=1, source_target_pairs={{0,16},{8,24},{16,0},{24,8},{1,17},{9,25},{17,1},{25,9},{2,18},{10... | collective-permute-start | bytes 2752520 | tf_op jit(solution)/shard_map/ppermute | solution.py:441
  632.7 6.4 collective-permute-start.37
  632.7 6.4 collective-permute-start.38
  633.2 5.9 collective-permute-start.39
  633.3 5.9 collective-permute-start.40
  (69 other events, 1302.1 us)
